TPU v7x, 128 devices: a whole 4x4x4 slice. The times are simulated.
128 devices in a mesh: gx: 8 (over z, core), gy: 16 (over x, y).
Axes of the slice: x: 4, y: 4, z: 4, core: 2. Of those that a mesh axis runs over, the one named last changes fastest.
Arguments:
- u_now: float32 [3, 40, 272, 256], P(None, 'gx', 'gy'), as said below
- load: float32 [3, 40, 272, 256], P(None, 'gx', 'gy'), may hold values from -6 to 6
- mass: float32 [40, 272, 256], P('gx', 'gy'), may hold values from 0.2 to 2
- modulus: float32 [32, 256, 256], P('gx', 'gy'), may hold values from 0.3 to 3
- plastic_ids: int32 [8, 16, 1024], P('gx', 'gy'), may hold values from 0 to 16383, as said below
- plastic_count: int32 [8, 16], P('gx', 'gy'), may hold values from 128 to 1024, as said below
- w_in: float32 [6, 512], replicated, may hold values from -2.5 to 2.5
- w_hidden: float32 [3, 512, 512], replicated, may hold values from -0.25 to 0.25
- w_head: float32 [512, 42], replicated, may hold values from -0.5 to 0.5
Outputs:
- increment: float32 [3, 40, 272, 256], P(None, 'gx', 'gy')
- cg_residual: float32 [3, 40, 272, 256], P(None, 'gx', 'gy')
Inputs may be any that keep to these rules, and one draw needn't show every extreme that they name: `u_now`: copies of one node in neighbouring blocks are equal, and nodes of the planes I = 32 and J = 256 are zero. `plastic_ids`: the entries of one block are distinct element indices of that block. `plastic_count`: some block holds 1024 live points in every draw.
All inputs are finite; a program needn't handle non-finite values.
Results may differ from a plain program's by a relative error of at most 0.0003.
Values sent between devices are 32-bit elements; how exact they have to be, the bound alone decides.
A program may use at most 128 MiB of HBM per device.

v0:
```python
import jax
import jax.numpy as jnp
from jax import lax
from jax.sharding import PartitionSpec as P

ITERS = 6


lame_first = 0.3 / (1.3 * 0.4)
lame_second = 1.0 / 2.6
highest = lax.Precision.HIGHEST


def with_halo(cells, sides, width):
    for axis, dim in sides:
        count = lax.axis_size(axis)
        ends = count - 1
        head = lax.slice_in_dim(cells, 0, width, axis=dim)
        tail = lax.slice_in_dim(cells, cells.shape[dim] - width, cells.shape[dim], axis=dim)
        cells = jnp.concatenate(
            [
                lax.ppermute(tail, axis, [(i, (i + 1) % count) for i in range(ends)]),
                cells,
                lax.ppermute(head, axis, [((i + 1) % count, i) for i in range(ends)]),
            ],
            axis=dim,
        )
    return cells


def pair_mean(values, dim):
    length = values.shape[dim]
    return 0.5 * (
        lax.slice_in_dim(values, 0, length - 1, axis=dim)
        + lax.slice_in_dim(values, 1, length, axis=dim)
    )


def pair_diff(values, dim):
    length = values.shape[dim]
    return lax.slice_in_dim(values, 1, length, axis=dim) - lax.slice_in_dim(
        values, 0, length - 1, axis=dim
    )


def strain_of(field):
    padded = jnp.pad(field, ((0, 0), (0, 0), (0, 0), (0, 1)))
    grad_x = pair_mean(pair_mean(pair_diff(padded, 1), 2), 3)
    grad_y = pair_mean(pair_mean(pair_diff(padded, 2), 1), 3)
    grad_z = pair_mean(pair_mean(pair_diff(padded, 3), 1), 2)
    parts = [
        grad_x[0],
        grad_y[1],
        grad_z[2],
        grad_z[1] + grad_y[2],
        grad_z[0] + grad_x[2],
        grad_y[0] + grad_x[1],
    ]
    return jnp.stack(parts).reshape(6, -1)


def iso_matrix():
    upper = lame_first * jnp.ones((3, 3), jnp.float32) + 2.0 * lame_second * jnp.eye(
        3, dtype=jnp.float32
    )
    lower = lame_second * jnp.eye(3, dtype=jnp.float32)
    zeros = jnp.zeros((3, 3), jnp.float32)
    return jnp.concatenate(
        [jnp.concatenate([upper, zeros], 1), jnp.concatenate([zeros, lower], 1)], 0
    )


def elastic_stress(strain, moduli):
    trace = strain[0] + strain[1] + strain[2]
    normal = lame_first * trace[None] + 2.0 * lame_second * strain[:3]
    shear = lame_second * strain[3:]
    return moduli[None] * jnp.concatenate([normal, shear], 0)


def contract(weights, values):
    return lax.dot_general(
        weights,
        values,
        (((0,), (0,)), ((), ())),
        precision=highest,
        preferred_element_type=jnp.float32,
    )


def surrogate(inputs, w_in, w_hidden, w_head):
    hidden = jnp.tanh(contract(w_in, inputs))
    for layer in range(w_hidden.shape[0]):
        hidden = jnp.tanh(contract(w_hidden[layer], hidden))
    return contract(w_head, hidden)


def tiled_surrogate(inputs, live_rows, w_in, w_hidden, w_head):
    total_rows = inputs.shape[1]
    tile_rows = min(256, total_rows)

    def advance(position, results):
        start = position * tile_rows
        block = lax.dynamic_slice_in_dim(inputs, start, tile_rows, 1)
        return lax.dynamic_update_slice_in_dim(
            results, surrogate(block, w_in, w_hidden, w_head), start, 1
        )

    turns = (live_rows + tile_rows - 1) // tile_rows
    return lax.fori_loop(0, turns, advance, jnp.zeros((42, total_rows), jnp.float32))


def plastic_laws(outputs, eps_plastic, modulus_plastic):
    iso = iso_matrix()
    stress_plastic = modulus_plastic[None] * (
        0.25 * jnp.dot(iso, eps_plastic, precision=highest) + outputs[:6]
    )
    factor = outputs[6:].reshape(6, 6, -1)
    outer = jnp.einsum("ikp,jkp->ijp", factor, factor, precision=highest)
    tangent = modulus_plastic[None, None] * (0.25 * iso[:, :, None] + outer / 6.0)
    return (stress_plastic, tangent)


def body(u_now, load, mass, modulus, plastic_ids, plastic_count, w_in, w_hidden, w_head):
    size_x = lax.axis_size("gx")
    size_y = lax.axis_size("gy")
    index_x = lax.axis_index("gx")
    index_y = lax.axis_index("gy")
    planes_x = u_now.shape[1]
    planes_y = u_now.shape[2]
    along_x = jnp.arange(planes_x)
    along_y = jnp.arange(planes_y)
    keep_x = jnp.where((along_x == planes_x - 1) & (index_x == size_x - 1), 0.0, 1.0)
    keep_y = jnp.where((along_y == planes_y - 1) & (index_y == size_y - 1), 0.0, 1.0)
    keep = (keep_x[:, None] * keep_y[None, :])[None, :, :, None].astype(jnp.float32)
    share_x = jnp.where(
        (along_x == 0) & (index_x > 0) | (along_x == planes_x - 1) & (index_x < size_x - 1),
        0.5,
        1.0,
    )
    share_y = jnp.where(
        (along_y == 0) & (index_y > 0) | (along_y == planes_y - 1) & (index_y < size_y - 1),
        0.5,
        1.0,
    )
    weight = (share_x[:, None] * share_y[None, :])[None, :, :, None].astype(jnp.float32)

    def inner(first, second):
        return jnp.sum(weight * first * second)

    def squared_norm(values):
        return lax.psum(inner(values, values), ("gx", "gy"))

    def assemble(local):
        rims = with_halo(local, (("gx", 1), ("gy", 2)), 1)
        total = local.at[:, 0].add(rims[:, 0, 1:-1]).at[:, -1].add(rims[:, -1, 1:-1])
        total = total.at[:, :, 0].add(rims[:, 1:-1, 0]).at[:, :, -1].add(rims[:, 1:-1, -1])
        total = total.at[:, 0, 0].add(rims[:, 0, 0]).at[:, 0, -1].add(rims[:, 0, -1])
        total = total.at[:, -1, 0].add(rims[:, -1, 0]).at[:, -1, -1].add(rims[:, -1, -1])
        return total * keep

    moduli = modulus.reshape(-1)
    element_ids = plastic_ids.reshape(-1)
    live_count = plastic_count.reshape(())
    slot_rows = element_ids.shape[0]
    live_mask = (jnp.arange(slot_rows) < live_count).astype(jnp.float32)
    strain_now = strain_of(u_now)
    eps_plastic = jnp.take(strain_now, element_ids, axis=1)
    modulus_plastic = jnp.take(moduli, element_ids)
    outputs = tiled_surrogate(eps_plastic, live_count, w_in, w_hidden, w_head)
    stress_plastic, tangent = plastic_laws(outputs, eps_plastic, modulus_plastic)

    def stress_of(strain, plastic_value):
        base = elastic_stress(strain, moduli)
        change = live_mask[None] * (plastic_value - jnp.take(base, element_ids, axis=1))
        return base.at[:, element_ids].add(change)

    _, pull_back = jax.vjp(strain_of, u_now)

    def forces(stress):
        return pull_back(stress)[0]

    residual = assemble(load - forces(stress_of(strain_now, stress_plastic)))
    increment = jnp.zeros_like(residual)
    direction = residual
    norm_now = squared_norm(residual)
    for step in range(ITERS):
        apply_strain = strain_of(direction)
        apply_local = jnp.einsum(
            "ijp,jp->ip", tangent, jnp.take(apply_strain, element_ids, axis=1), precision=highest
        )
        image = assemble(forces(stress_of(apply_strain, apply_local)) + mass[None] * direction)
        alpha = norm_now / lax.psum(inner(direction, image), ("gx", "gy"))
        increment = increment + alpha * direction
        residual = residual - alpha * image
        norm_next = squared_norm(residual)
        direction = residual + norm_next / norm_now * direction
        norm_now = norm_next
    return (increment, residual)


def solution(mesh):
    return jax.shard_map(
        body,
        mesh=mesh,
        in_specs=(
            P(None, "gx", "gy", None),
            P(None, "gx", "gy", None),
            P("gx", "gy", None),
            P("gx", "gy", None),
            P("gx", "gy", None),
            P("gx", "gy"),
            P(),
            P(),
            P(),
        ),
        out_specs=(P(None, "gx", "gy", None), P(None, "gx", "gy", None)),
        check_vma=False,
    )
```

profile of v0, /device:TPU:1, one launch (start us, length us, event | category | flops | bytes accessed | tf_op | source)
XLA Modules:
  0.0 1593.2 jit_solution(2232179336602801178)
XLA Ops:
  69.5 12.3 scatter_fusion
  81.9 33.3 %slice_reduce_fusion.39 = (f32[16384]{0:T(1024)S(1)}, f32[16384]{0:T(1024)S(1)}, f32[16384]{0:T(1024)S(1)}, f32[16384]{0:T(1024)S(1)}, f32[16384]{0:T(1024)S(1)}, /*index=5*/f32[16384]{0:T(1024)S(1)}) fusion(f32[6,16384]{0,1:T(8,128)} %scatter_fusion), kind=kLoop, calls=%fused_computation.75 | loop fusion | bytes 786432 | tf_op jit(solution)/shard_map/transpose(jvp())/unstack | solution.py:59
  124.9 12.6 fusion.9
  198.1 12.2 scatter_fusion.1
  210.4 33.3 %slice_reduce_fusion.33 = (f32[16384]{0:T(1024)S(1)}, f32[16384]{0:T(1024)S(1)}, f32[16384]{0:T(1024)S(1)}, f32[16384]{0:T(1024)S(1)}, f32[16384]{0:T(1024)S(1)}, /*index=5*/f32[16384]{0:T(1024)S(1)}) fusion(f32[6,16384]{0,1:T(8,128)} %scatter_fusion.1), kind=kLoop, calls=%fused_computation.69 | loop fusion | bytes 786432 | tf_op jit(solution)/shard_map/transpose(jvp())/unstack | solution.py:59
  267.7 76.3 %all-reduce.198 = (f32[]{:T(128)}, f32[]{:T(128)}) all-reduce(f32[]{:T(128)} %get-tuple-element.782, f32[]{:T(128)} %get-tuple-element.781), channel_id=1, replica_groups=mesh['gx'=8,'gy'=16] {'gx','gy'}, use_global_device_ids=true, to_apply=%region_5.7 | all-reduce | flops 2 | bytes 16 | tf_op jit(solution)/shard_map/psum | solution.py:151
  346.2 63.6 %psum.86 = f32[]{:T(128)} all-reduce(f32[]{:T(128)} %fusion.24), channel_id=1, replica_groups=mesh['gx'=8,'gy'=16] {'gx','gy'}, use_global_device_ids=true, to_apply=%region_10.12 | all-reduce | flops 1 | bytes 8 | tf_op jit(solution)/shard_map/psum | solution.py:151
  466.3 33.3 %slice_reduce_fusion.27 = (f32[16384]{0:T(1024)S(1)}, f32[16384]{0:T(1024)S(1)}, f32[16384]{0:T(1024)S(1)}, f32[16384]{0:T(1024)S(1)}, f32[16384]{0:T(1024)S(1)}, /*index=5*/f32[16384]{0:T(1024)S(1)}) fusion(f32[6,16384]{0,1:T(8,128)} %scatter_fusion.2), kind=kLoop, calls=%fused_computation.63 | loop fusion | bytes 786432 | tf_op jit(solution)/shard_map/transpose(jvp())/unstack | solution.py:59
  522.0 66.6 %psum.87 = f32[]{:T(128)} all-reduce(f32[]{:T(128)} %multiply_reduce_fusion.4), channel_id=1, replica_groups=mesh['gx'=8,'gy'=16] {'gx','gy'}, use_global_device_ids=true, to_apply=%region_13.15 | all-reduce | flops 1 | bytes 8 | tf_op jit(solution)/shard_map/psum | solution.py:192
  590.8 63.4 %psum.88 = f32[]{:T(128)} all-reduce(f32[]{:T(128)} %get-tuple-element.805), channel_id=1, replica_groups=mesh['gx'=8,'gy'=16] {'gx','gy'}, use_global_device_ids=true, to_apply=%region_15.17 | all-reduce | flops 1 | bytes 8 | tf_op jit(solution)/shard_map/psum | solution.py:151
  699.0 12.4 scatter_fusion.3
  711.4 33.3 %slice_reduce_fusion.21 = (f32[16384]{0:T(1024)S(1)}, f32[16384]{0:T(1024)S(1)}, f32[16384]{0:T(1024)S(1)}, f32[16384]{0:T(1024)S(1)}, f32[16384]{0:T(1024)S(1)}, /*index=5*/f32[16384]{0:T(1024)S(1)}) fusion(f32[6,16384]{0,1:T(8,128)} %scatter_fusion.3), kind=kLoop, calls=%fused_computation.57 | loop fusion | bytes 786432 | tf_op jit(solution)/shard_map/transpose(jvp())/unstack | solution.py:59
  766.8 66.6 %psum.89 = f32[]{:T(128)} all-reduce(f32[]{:T(128)} %multiply_reduce_fusion.3), channel_id=1, replica_groups=mesh['gx'=8,'gy'=16] {'gx','gy'}, use_global_device_ids=true, to_apply=%region_18.20 | all-reduce | flops 1 | bytes 8 | tf_op jit(solution)/shard_map/psum | solution.py:192
  835.5 63.2 %psum.90 = f32[]{:T(128)} all-reduce(f32[]{:T(128)} %get-tuple-element.803), channel_id=1, replica_groups=mesh['gx'=8,'gy'=16] {'gx','gy'}, use_global_device_ids=true, to_apply=%region_20.22 | all-reduce | flops 1 | bytes 8 | tf_op jit(solution)/shard_map/psum | solution.py:151
  957.3 33.3 %slice_reduce_fusion.15 = (f32[16384]{0:T(1024)S(1)}, f32[16384]{0:T(1024)S(1)}, f32[16384]{0:T(1024)S(1)}, f32[16384]{0:T(1024)S(1)}, f32[16384]{0:T(1024)S(1)}, /*index=5*/f32[16384]{0:T(1024)S(1)}) fusion(f32[6,16384]{0,1:T(8,128)} %scatter_fusion.4), kind=kLoop, calls=%fused_computation.51 | loop fusion | bytes 786432 | tf_op jit(solution)/shard_map/transpose(jvp())/unstack | solution.py:59
  1012.7 66.7 %psum.91 = f32[]{:T(128)} all-reduce(f32[]{:T(128)} %multiply_reduce_fusion.2), channel_id=1, replica_groups=mesh['gx'=8,'gy'=16] {'gx','gy'}, use_global_device_ids=true, to_apply=%region_23.25 | all-reduce | flops 1 | bytes 8 | tf_op jit(solution)/shard_map/psum | solution.py:192
  1081.6 63.3 %psum.92 = f32[]{:T(128)} all-reduce(f32[]{:T(128)} %get-tuple-element.801), channel_id=1, replica_groups=mesh['gx'=8,'gy'=16] {'gx','gy'}, use_global_device_ids=true, to_apply=%region_25.27 | all-reduce | flops 1 | bytes 8 | tf_op jit(solution)/shard_map/psum | solution.py:151
  1198.9 12.6 scatter_fusion.5
  1211.5 33.3 %slice_reduce_fusion.9 = (f32[16384]{0:T(1024)S(1)}, f32[16384]{0:T(1024)S(1)}, f32[16384]{0:T(1024)S(1)}, f32[16384]{0:T(1024)S(1)}, f32[16384]{0:T(1024)S(1)}, /*index=5*/f32[16384]{0:T(1024)S(1)}) fusion(f32[6,16384]{0,1:T(8,128)} %scatter_fusion.5), kind=kLoop, calls=%fused_computation.45 | loop fusion | bytes 786432 | tf_op jit(solution)/shard_map/transpose(jvp())/unstack | solution.py:59
  1267.2 66.6 %psum.93 = f32[]{:T(128)} all-reduce(f32[]{:T(128)} %multiply_reduce_fusion.1), channel_id=1, replica_groups=mesh['gx'=8,'gy'=16] {'gx','gy'}, use_global_device_ids=true, to_apply=%region_28.30 | all-reduce | flops 1 | bytes 8 | tf_op jit(solution)/shard_map/psum | solution.py:192
  1335.8 63.3 %psum.94 = f32[]{:T(128)} all-reduce(f32[]{:T(128)} %get-tuple-element.799), channel_id=1, replica_groups=mesh['gx'=8,'gy'=16] {'gx','gy'}, use_global_device_ids=true, to_apply=%region_30.32 | all-reduce | flops 1 | bytes 8 | tf_op jit(solution)/shard_map/psum | solution.py:151
  1455.3 12.2 scatter_fusion.6
  1467.5 33.3 %slice_reduce_fusion.3 = (f32[16384]{0:T(1024)S(1)}, f32[16384]{0:T(1024)S(1)}, f32[16384]{0:T(1024)S(1)}, f32[16384]{0:T(1024)S(1)}, f32[16384]{0:T(1024)S(1)}, /*index=5*/f32[16384]{0:T(1024)S(1)}) fusion(f32[6,16384]{0,1:T(8,128)} %scatter_fusion.6), kind=kLoop, calls=%fused_computation.39 | loop fusion | bytes 786432 | tf_op jit(solution)/shard_map/transpose(jvp())/unstack | solution.py:59
  1522.9 66.4 %psum.95 = f32[]{:T(128)} all-reduce(f32[]{:T(128)} %multiply_reduce_fusion), channel_id=1, replica_groups=mesh['gx'=8,'gy'=16] {'gx','gy'}, use_global_device_ids=true, to_apply=%region_33.35 | all-reduce | flops 1 | bytes 8 | tf_op jit(solution)/shard_map/psum | solution.py:192
  (600 shorter events, 550.8 us)
Async XLA Ops:
  116.3 21.9 %collective-permute-start = (f32[3,1,17,256]{3,2,1,0:T(8,128)S(1)}, f32[3,1,17,256]{3,2,1,0:T(8,128)S(1)}, u32[]{:S(2)}, u32[]{:S(2)}) collective-permute-start(f32[3,1,17,256]{3,2,1,0:T(8,128)S(1)} %slice.2804), channel_id=1, source_target_pairs={{0,16},{16,32},{32,48},{48,64},{64,80},{80,96},{96,112},{1,17},{17... | collective-permute-start | bytes 156680 | tf_op jit(solution)/shard_map/ppermute | solution.py:22
  138.2 5.7 collective-permute-start.1
  143.9 4.5 collective-permute-start.2
  147.1 4.5 collective-permute-start.3
  244.7 4.7 collective-permute-start.4
  249.4 6.3 collective-permute-start.5
  255.8 4.5 collective-permute-start.6
  259.0 4.5 collective-permute-start.7
  500.6 5.0 collective-permute-start.8
  505.7 6.3 collective-permute-start.9
  513.3 4.5 collective-permute-start.11
  745.8 4.4 collective-permute-start.12
  750.2 6.3 collective-permute-start.13
  756.5 2.9 collective-permute-start.14
  758.1 4.5 collective-permute-start.15
  991.7 4.6 collective-permute-start.16
  996.3 6.3 collective-permute-start.17
  1004.0 4.5 collective-permute-start.19
  1245.8 4.9 collective-permute-start.20
  1250.8 6.3 collective-permute-start.21
  1258.4 4.5 collective-permute-start.23
  1501.9 4.7 collective-permute-start.24
  1506.5 6.3 collective-permute-start.25
  1514.2 4.5 collective-permute-start.27
  (17 other events, 287.4 us)
where the time goes:
time: 1610 us; the launch traced here: 1590 us
  blocking collectives  726 us (45%)
  local copies, waits for them, and re-layouts  462 us (29%)
  other arithmetic  187 us (12%)
  matrix products  77.4 us (5%)
  starting transfers between devices  60.6 us (4%)
  waiting for transfers between devices  59.7 us (4%)
  between operations  20.2 us (1%)
    psum x6, blocking collectives, squared_norm(): return lax.psum(inner(values, values), ('gx', 'gy'))  393 us
    psum x5, blocking collectives, body(): alpha = norm_now / lax.psum(inner(direction, image), ('gx', 'gy'))  333 us
    another operation x63, local copies, waits for them, and re-layouts, strain_of(): return jnp.stack(parts).reshape(6, -1)  280 us
    scatter-add x7, other arithmetic, stress_of(): return base.at[:, element_ids].add(change)  86.1 us
    mul x7, other arithmetic, elastic_stress(): return moduli[None] * jnp.concatenate([normal, shear], 0)  55.3 us
    dot_general x6, matrix products, body(): jnp.einsum('ijp,jp->ip', tangent, jnp.take(apply_strain, element_ids, axi...  52.6 us
    ppermute x14, waiting for transfers between devices, with_halo(): lax.ppermute(head, axis, [((i + 1) % count, i) for i in range(ends)])  51.5 us
    gather x14, local copies, waits for them, and re-layouts, stress_of(): jnp.take(base, element_ids, axis=1)  46.8 us
  transfers between devices with their start and end apart: 28, of which 20 were waited for; matrix products, arithmetic and copies ran while one was open for 1% of the time, Pallas kernels for 0%

commit v1 on v0

v1 whole, which is shorter than its diff:
```python
import jax
import jax.numpy as jnp
from jax import lax
from jax.experimental import pallas as pl
from jax.experimental.pallas import tpu as pltpu
from jax.sharding import PartitionSpec as P

MESH = pl.DeviceIdType.MESH
F32, BF16 = jnp.float32, jnp.bfloat16
LAME_FIRST = 0.3 / (1.3 * 0.4)
LAME_SECOND = 1.0 / 2.6

BX, BY, NZ = 4, 16, 256
NODES_X, NODES_Y = BX + 1, BY + 1
ROWS = BY + 3
SUB = 8
SLOTS, HID, HIDDEN_LAYERS = 1024, 512, 3
COLUMNS = BY * BX
OUTER = 3
CHUNK = 256
GROUP = 7

PAIRS = [(a, b) for a in range(6) for b in range(a, 6)]
PAIR_OF = {}
for _at, (_a, _b) in enumerate(PAIRS):
    PAIR_OF[_a, _b] = PAIR_OF[_b, _a] = _at
N_PAIRS = len(PAIRS)
N_SCATTER = 28

DIRECTIONS = [(dx, dy) for dx in (-1, 0, 1) for dy in (-1, 0, 1) if (dx, dy) != (0, 0)]


def iso(a, b):
    if a < 3 and b < 3:
        return LAME_FIRST + (2.0 * LAME_SECOND if a == b else 0.0)
    return LAME_SECOND if a == b else 0.0


def z_next(values):
    lane = lax.broadcasted_iota(jnp.int32, values.shape, 1)
    return jnp.where(lane == NZ - 1, 0.0, pltpu.roll(values, NZ - 1, 1))


def z_prev(values):
    lane = lax.broadcasted_iota(jnp.int32, values.shape, 1)
    return jnp.where(lane == 0, 0.0, pltpu.roll(values, 1, 1))


def x_pairs(values):
    upper = pltpu.roll(values, SUB - 1, 0)
    return upper + values, upper - values


def strain_row(low, high):
    a = [low[m][1] + high[m][1] for m in range(3)]
    b = [high[m][0] - low[m][0] for m in range(3)]
    c = [high[m][0] + low[m][0] for m in range(3)]
    yz, xz, xy = c[1] + b[2], c[0] + a[2], b[0] + a[1]
    return [
        z_next(a[0]) + a[0],
        z_next(b[1]) + b[1],
        z_next(c[2]) - c[2],
        z_next(yz) + (b[2] - c[1]),
        z_next(xz) + (a[2] - c[0]),
        z_next(xy) + xy,
    ]


def force_parts(stress):
    before = [z_prev(s) for s in stress]
    total = {n: stress[n] + before[n] for n in (0, 1, 3, 4, 5)}
    differ = {n: before[n] - stress[n] for n in (2, 3, 4)}
    parts = []
    for along_x, along_y, along_z in ((0, 5, 4), (5, 1, 3), (4, 3, 2)):
        parts.append(
            (
                total[along_x],
                differ[along_z] - total[along_y],
                differ[along_z] + total[along_y],
            )
        )
    return parts


def force_of(along_x, other):
    return pltpu.roll(along_x + other, 1, 0) + (other - along_x)


def split(values):
    high = values.astype(BF16)
    return high, (values - high.astype(F32)).astype(BF16)


def mm(a, b):
    return jnp.dot(a, b, preferred_element_type=F32)


def face(dx, dy, depth):
    if depth == 2:
        sx = {-1: slice(1, 3), 0: slice(1, 6), 1: slice(4, 6)}[dx]
        tx = {-1: slice(5, 7), 0: slice(1, 6), 1: slice(0, 2)}[dx]
        sy = {-1: slice(1, 3), 0: slice(1, 18), 1: slice(16, 18)}[dy]
        ty = {-1: slice(17, 19), 0: slice(1, 18), 1: slice(0, 2)}[dy]
    else:
        sx = {-1: slice(2, 3), 0: slice(1, 6), 1: slice(4, 5)}[dx]
        tx = {-1: slice(6, 7), 0: slice(1, 6), 1: slice(0, 1)}[dx]
        sy = {-1: slice(2, 3), 0: slice(1, 18), 1: slice(16, 17)}[dy]
        ty = {-1: slice(18, 19), 0: slice(1, 18), 1: slice(0, 1)}[dy]
    return sy, sx, ty, tx


def element_face(dx, dy):
    sx = {-1: slice(1, 2), 0: slice(1, 5), 1: slice(4, 5)}[dx]
    tx = {-1: slice(5, 6), 0: slice(1, 5), 1: slice(0, 1)}[dx]
    sy = {-1: slice(0, 1), 0: slice(0, 16), 1: slice(15, 16)}[dy]
    ty = {-1: slice(17, 18), 0: slice(1, 17), 1: slice(0, 1)}[dy]
    return sy, sx, ty, tx


def kernel(
    size_x, size_y,
    u_hbm, load_hbm, mass_hbm, modulus_hbm, ids_ref, count_ref, w_in_ref, w_hidden_hbm, w_head_ref,
    increment_hbm, residual_hbm,
    ux, lx, mass_part, mass_full, mass_rx, modulus, weights,
    strain_now, onehot_k, onehot_kt, onehot_r, onehot_r8, inputs_t, out_t, values, lhs, scattered,
    own_tangent, tangent, tangent_rx,
    v0, v1, v2, q1, q0, d1, x, sum_rx, copy_rx, gathered,
    load_sem, out_sem, mass_send, mass_recv, tan_send, tan_recv,
    sum_send, sum_recv, copy_send, copy_recv, all_send, all_recv,
):
    index_x, index_y = lax.axis_index("gx"), lax.axis_index("gy")
    me = index_x * size_y + index_y
    peers = size_x * size_y
    neighbours = [
        (lax.rem(index_x + dx + size_x, size_x), lax.rem(index_y + dy + size_y, size_y))
        for dx, dy in DIRECTIONS
    ]

    def peer(step):
        other = lax.rem(me + step, peers)
        return (other // size_y, lax.rem(other, size_y))

    barrier = pltpu.get_barrier_semaphore()

    def greet(step, carry):
        pl.semaphore_signal(barrier, inc=1, device_id=peer(step), device_id_type=MESH)
        return carry

    lax.fori_loop(1, peers, greet, 0)

    for ref in (ux, lx, mass_part, modulus):
        ref[...] = jnp.zeros_like(ref)
    loads = []
    for i in range(NODES_X):
        loads.append(pltpu.make_async_copy(u_hbm.at[:, i], ux.at[:, 1:18, i + 1], load_sem.at[0, i]))
    for i in range(BX):
        loads.append(pltpu.make_async_copy(modulus_hbm.at[i], modulus.at[:, i + 1], load_sem.at[1, i]))
    for i in range(NODES_X):
        loads.append(pltpu.make_async_copy(mass_hbm.at[i], mass_part.at[1:18, i + 1], load_sem.at[2, i]))
        loads.append(pltpu.make_async_copy(load_hbm.at[:, i], lx.at[:, 1:18, i + 1], load_sem.at[3, i]))
    for layer in range(HIDDEN_LAYERS):
        loads.append(pltpu.make_async_copy(w_hidden_hbm.at[layer], weights.at[layer], load_sem.at[4, layer]))
    for copy in loads:
        copy.start()
    for ref in (q1, q0, d1, x):
        ref[...] = jnp.zeros_like(ref)

    ids = ids_ref[...]
    slot = lax.broadcasted_iota(jnp.int32, (1, SLOTS), 1)
    live = jnp.where(slot < count_ref[0, 0], 1.0, 0.0)
    at_k = ids & (NZ - 1)
    at_j = (ids >> 8) & (BY - 1)
    at_i = ids >> 12
    onehot_k[...] = jnp.where(
        lax.broadcasted_iota(jnp.int32, (NZ, SLOTS), 0) == at_k, 1.0, 0.0
    ).astype(BF16)
    onehot_r[...] = jnp.where(
        lax.broadcasted_iota(jnp.int32, (COLUMNS, SLOTS), 0) == at_j * BX + at_i, live, 0.0
    ).astype(BF16)
    onehot_r8[...] = jnp.where(
        lax.broadcasted_iota(jnp.int32, (BY * SUB, SLOTS), 0) == at_j * SUB + at_i + 1, 1.0, 0.0
    )
    k_column = jnp.broadcast_to(at_k.astype(F32), (128, SLOTS)).T
    lane_k = lax.broadcasted_iota(jnp.int32, (SLOTS, 128), 1).astype(F32)
    onehot_kt[:, 0:128] = jnp.where(k_column == lane_k, 1.0, 0.0).astype(BF16)
    onehot_kt[:, 128:256] = jnp.where(k_column == lane_k + 128.0, 1.0, 0.0).astype(BF16)

    for copy in loads:
        copy.wait()

    def pairs_of(ref, row):
        return [x_pairs(ref[m, row]) for m in range(3)]

    def strain_step(row, low):
        high = pairs_of(ux, row + 1)
        for n, value in enumerate(strain_row(low, high)):
            strain_now[n, row - 1] = 0.25 * value
        return high

    lax.fori_loop(1, 1 + BY, strain_step, pairs_of(ux, 1))

    picked = []
    for n in range(6):
        high, low = split(strain_now[n].reshape(BY * SUB, NZ))
        rows = mm(high, onehot_k[...]) + mm(low, onehot_k[...])
        picked.append(jnp.sum(rows * onehot_r8[...], axis=0, keepdims=True))
    eps = jnp.concatenate(picked + [jnp.zeros((2, SLOTS), F32)], axis=0)
    eps_high = eps.astype(BF16).astype(F32)
    stacked = jnp.concatenate(
        [eps_high, eps - eps_high, eps_high, jnp.zeros((104, SLOTS), F32)], axis=0
    )
    inputs_t[...] = stacked.T.astype(BF16)

    w_in = jnp.concatenate([w_in_ref[...], jnp.zeros((2, HID), F32)], axis=0)
    w_in_high = w_in.astype(BF16).astype(F32)
    w_first = jnp.concatenate(
        [w_in_high, w_in_high, w_in - w_in_high, jnp.zeros((104, HID), F32)], axis=0
    ).astype(BF16)
    from_out = lax.broadcasted_iota(jnp.int32, (42, 128), 0)
    to_lane = lax.broadcasted_iota(jnp.int32, (42, 128), 1)
    place = jnp.where(
        (from_out == (to_lane // 8) * 6 + to_lane % 8) & (to_lane % 8 < 6) & (to_lane < 56), 1.0, 0.0
    ).astype(BF16)
    head_high, head_low = split(w_head_ref[...])
    head_high = mm(head_high, place).astype(BF16)
    head_low = mm(head_low, place).astype(BF16)
    halves = [split(weights[layer]) for layer in range(HIDDEN_LAYERS)]

    def surrogate_chunk(at, carry):
        start = pl.multiple_of(at * CHUNK, CHUNK)
        hidden = jnp.tanh(mm(inputs_t[pl.ds(start, CHUNK)], w_first))
        for w_high, w_low in halves:
            high, low = split(hidden)
            hidden = jnp.tanh(mm(high, w_high) + (mm(low, w_high) + mm(high, w_low)))
        high, low = split(hidden)
        out = mm(high, head_high) + (mm(low, head_high) + mm(high, head_low))
        out_t[:, pl.ds(start, CHUNK)] = out.T
        return carry

    lax.fori_loop(0, SLOTS // CHUNK, surrogate_chunk, 0)

    pl.semaphore_wait(barrier, peers - 1)
    mass_copies = []
    for q, ((dx, dy), device) in enumerate(zip(DIRECTIONS, neighbours)):
        sy, sx, ty, tx = face(dx, dy, 2)
        kind = 0 if dy == 0 else (1 if dx == 0 else 2)
        copy = pltpu.make_async_remote_copy(
            mass_part.at[sy, sx], mass_rx.at[kind, ty, tx], mass_send.at[q], mass_recv.at[q],
            device_id=device, device_id_type=MESH,
        )
        copy.start()
        mass_copies.append(copy)

    factor = [out_t[8 * (a + 1) : 8 * (a + 2)] for a in range(6)]
    for at, (a, b) in enumerate(PAIRS):
        values[at : at + 1] = jnp.sum(factor[a] * factor[b], axis=0, keepdims=True) * (1.0 / 6.0)
    values[N_PAIRS : N_PAIRS + 6] = out_t[0:6]
    values[N_SCATTER - 1 : N_SCATTER] = jnp.ones((1, SLOTS), F32)

    def scatter_group(at, carry):
        for n in range(GROUP):
            high, low = split(values[pl.ds(at * GROUP + n, 1)])
            rows = onehot_r[...]
            lhs[n * COLUMNS : (n + 1) * COLUMNS] = rows * high
            lhs[(GROUP + n) * COLUMNS : (GROUP + n + 1) * COLUMNS] = rows * low
        spread = mm(lhs[...], onehot_kt[...])
        spread = spread[: GROUP * COLUMNS] + spread[GROUP * COLUMNS :]
        sub = lax.broadcasted_iota(jnp.int32, (SUB, NZ), 0)
        inside = (sub >= 1) & (sub <= BX)
        for n in range(GROUP):
            for g in range(BY // 2):
                start = n * COLUMNS + g * SUB
                both = spread[start : start + SUB]
                scattered[at * GROUP + n, 2 * g] = jnp.where(inside, pltpu.roll(both, 1, 0), 0.0)
                scattered[at * GROUP + n, 2 * g + 1] = jnp.where(inside, pltpu.roll(both, 5, 0), 0.0)
        return carry

    lax.fori_loop(0, N_SCATTER // GROUP, scatter_group, 0)

    def tangent_row(row, carry):
        scale = modulus[row]
        base = scale * (1.0 - 0.75 * scattered[N_SCATTER - 1, row])
        for at, (a, b) in enumerate(PAIRS):
            entry = scale * scattered[at, row]
            if iso(a, b):
                entry = entry + base * iso(a, b)
            own_tangent[at, row] = entry * (1.0 / 16.0)
        return carry

    lax.fori_loop(0, BY, tangent_row, 0)

    tangent_copies = []
    for q, ((dx, dy), device) in enumerate(zip(DIRECTIONS, neighbours)):
        sy, sx, ty, tx = element_face(dx, dy)
        copy = pltpu.make_async_remote_copy(
            own_tangent.at[:, sy, sx], tangent_rx.at[:, ty, tx], tan_send.at[q], tan_recv.at[q],
            device_id=device, device_id_type=MESH,
        )
        copy.start()
        tangent_copies.append(copy)

    def sum_copies(parity):
        copies = []
        for q, ((dx, dy), device) in enumerate(zip(DIRECTIONS, neighbours)):
            sy, sx, ty, tx = face(dx, dy, 2)
            kind = 0 if dy == 0 else (1 if dx == 0 else 2)
            copies.append(
                pltpu.make_async_remote_copy(
                    v2.at[:, sy, sx], sum_rx.at[parity, kind, :, ty, tx],
                    sum_send.at[parity, q], sum_recv.at[parity, q],
                    device_id=device, device_id_type=MESH,
                )
            )
        return copies

    def exact_copies(parity):
        copies = []
        for q, ((dx, dy), device) in enumerate(zip(DIRECTIONS, neighbours)):
            sy, sx, ty, tx = face(dx, dy, 1)
            copies.append(
                pltpu.make_async_remote_copy(
                    v1.at[:, sy, sx], copy_rx.at[parity, :, ty, tx],
                    copy_send.at[parity, q], copy_recv.at[parity, q],
                    device_id=device, device_id_type=MESH,
                )
            )
        return copies

    sub = lax.broadcasted_iota(jnp.int32, (SUB, NZ), 0)
    global_x = index_x * BX + sub - 1
    keep_x = jnp.where(
        (global_x >= 0) & (global_x < size_x * BX) & (sub < SUB - 1), 1.0, 0.0
    )
    own_planes = (sub >= 1) & (sub <= NODES_X)
    rim_planes = ((sub <= 1) & (index_x > 0)) | ((sub >= NODES_X) & (sub <= NODES_X + 1))
    all_planes = sub <= NODES_X + 1

    def keep_of(row):
        global_y = index_y * BY + row - 1
        inside = jnp.where((global_y >= 0) & (global_y < size_y * BY), 1.0, 0.0)
        return keep_x * inside

    def assembled(part, side, flank, corner, row):
        own_row = (row >= 1) & (row <= NODES_Y)
        rim_row = ((row <= 1) & (index_y > 0)) | (row >= NODES_Y)
        total = jnp.where(own_planes & own_row, part, 0.0)
        total = total + jnp.where(rim_planes & own_row, side, 0.0)
        total = total + jnp.where(own_planes & rim_row, flank, 0.0)
        return total + jnp.where(rim_planes & rim_row, corner, 0.0)

    def stress_now(row):
        scale = 0.25 * modulus[row]
        base = scale * (1.0 - 0.75 * scattered[N_SCATTER - 1, row])
        eps_row = [strain_now[n, row] for n in range(6)]
        trace = LAME_FIRST * (eps_row[0] + eps_row[1] + eps_row[2])
        elastic = [trace + 2.0 * LAME_SECOND * eps_row[n] for n in range(3)]
        elastic += [LAME_SECOND * eps_row[n] for n in range(3, 6)]
        return [base * elastic[n] + scale * scattered[N_PAIRS + n, row] for n in range(6)]

    zero = jnp.zeros((SUB, NZ), F32)
    no_parts = [(zero, zero)] * 3

    def residual_step(row, before):
        parts = force_parts(stress_now(row - 1))
        for m in range(3):
            force = force_of(parts[m][0] + before[m][0], parts[m][1] + before[m][1])
            v2[m, row] = lx[m, row] - force
        return [(parts[m][0], parts[m][2]) for m in range(3)]

    last = lax.fori_loop(1, 1 + BY, residual_step, no_parts)
    for m in range(3):
        v2[m, NODES_Y] = lx[m, NODES_Y] - force_of(*last[m])

    first_copies = sum_copies(0)
    for copy in first_copies:
        copy.start()
    for copy in mass_copies:
        copy.wait()

    def mass_row(row, carry):
        mass_full[row] = assembled(
            mass_part[row], mass_rx[0, row], mass_rx[1, row], mass_rx[2, row], row
        )
        return carry

    lax.fori_loop(0, ROWS, mass_row, 0)
    for copy in first_copies:
        copy.wait()

    def start_row(row, carry):
        keep = keep_of(row)
        for m in range(3):
            v0[m, row] = keep * assembled(
                v2[m, row], sum_rx[0, 0, m, row], sum_rx[0, 1, m, row], sum_rx[0, 2, m, row], row
            )
        return carry

    lax.fori_loop(0, ROWS, start_row, 0)
    for copy in tangent_copies:
        copy.wait()

    def merge_row(row, carry):
        own_row = (row >= 1) & (row <= BY)
        own = (sub >= 1) & (sub <= BX) & own_row
        inside = (global_x >= 0) & (sub <= BX + 1) & (index_y * BY + row - 1 >= 0)
        from_row = jnp.clip(row - 1, 0, BY - 1)
        for at in range(N_PAIRS):
            entry = jnp.where(own, own_tangent[at, from_row], tangent_rx[at, row])
            tangent[at, row] = jnp.where(inside, entry, 0.0)
        return carry

    lax.fori_loop(0, BY + 2, merge_row, 0)

    def stress_row(ref, row, strain):
        entries = [ref[at, row] for at in range(N_PAIRS)]
        result = []
        for a in range(6):
            total = entries[PAIR_OF[a, 0]] * strain[0]
            for b in range(1, 6):
                total = total + entries[PAIR_OF[a, b]] * strain[b]
            result.append(total)
        return result

    def first_image(row, carry):
        low, before = carry
        high = pairs_of(v0, row + 1)
        parts = force_parts(stress_row(tangent, row, strain_row(low, high)))

        @pl.when(row > 0)
        def _():
            keep = keep_of(row)
            for m in range(3):
                force = force_of(parts[m][0] + before[m][0], parts[m][1] + before[m][1])
                v1[m, row] = keep * (force + mass_full[row] * v0[m, row])

        return high, [(parts[m][0], parts[m][2]) for m in range(3)]

    def second_image(row, carry):
        low, before, sums = carry
        high = pairs_of(v1, row + 1)
        parts = force_parts(stress_row(own_tangent, row - 1, strain_row(low, high)))
        rr, r_ar, ar_ar, ar_aar = sums
        for m in range(3):
            here, image = v0[m, row], v1[m, row]
            force = force_of(parts[m][0] + before[m][0], parts[m][1] + before[m][1])
            force = force + mass_part[row] * image
            v2[m, row] = force
            rr = rr + here * here
            r_ar = r_ar + here * image
            ar_ar = ar_ar + image * image
            ar_aar = ar_aar + image * force
        return high, [(parts[m][0], parts[m][2]) for m in range(3)], (rr, r_ar, ar_ar, ar_aar)

    unique_planes = (sub >= 1) & (sub <= BX)
    lane = lax.broadcasted_iota(jnp.int32, (1, 128), 1)

    def outer(step, carry):
        be0, ia1, ia0, rr_before = carry
        parity = lax.rem(step, 2)
        sum_parity = lax.rem(step + 1, 2)
        lax.fori_loop(0, BY + 2, first_image, (pairs_of(v0, 0), no_parts))
        exact = exact_copies(parity)
        for copy in exact:
            copy.start()
        _, before, sums = lax.fori_loop(
            1, 1 + BY, second_image, (pairs_of(v1, 1), no_parts, (zero,) * 4)
        )
        ar_aar = sums[3]
        for m in range(3):
            image = v1[m, NODES_Y]
            force = force_of(*before[m]) + mass_part[NODES_Y] * image
            v2[m, NODES_Y] = force
            ar_aar = ar_aar + jnp.where(own_planes, image * force, 0.0)
        summed = sum_copies(sum_parity)
        for copy in summed:
            copy.start()

        message = jnp.zeros((1, 128), F32)
        for at, (value, mask) in enumerate(
            ((sums[0], unique_planes), (sums[1], unique_planes), (sums[2], unique_planes), (ar_aar, own_planes))
        ):
            total = jnp.sum(jnp.where(mask, value, 0.0), axis=0, keepdims=True)
            total = jnp.sum(total, axis=1, keepdims=True)
            message = message + jnp.where(lane == at, total, 0.0)
        gathered[parity, me] = message

        def tell(other, unused):
            pltpu.make_async_remote_copy(
                gathered.at[parity, me], gathered.at[parity, me],
                all_send.at[parity], all_recv.at[parity],
                device_id=peer(other), device_id_type=MESH,
            ).start()
            return unused

        lax.fori_loop(1, peers, tell, 0)
        for copy in exact + summed:
            copy.wait()
        rest = gathered.at[parity, 0 : peers - 1]
        pltpu.make_async_copy(rest, rest, all_recv.at[parity]).wait()
        totals = jnp.sum(gathered[parity], axis=0)
        rr2, m1, m2, m3 = [
            jnp.sum(jnp.where(lane == at, totals, 0.0), axis=1, keepdims=True) for at in range(4)
        ]
        be1 = jnp.where(step == 0, 0.0, rr2 / rr_before)
        r_q1 = -rr2 * ia1
        ar_q1 = (r_q1 - m1) * ia1
        q1_q1 = (rr_before + rr2) * ia1 * ia1
        ar_q0 = rr2 * ia1 * ia0
        q1_q0 = -rr_before * ia1 * ia0
        q1_aar = ia1 * (ar_q1 - be0 * ar_q0 - m2)
        q1_aq1 = ia1 * (q1_q1 - be0 * q1_q0 - ar_q1)
        q2_q2 = m2 + 2.0 * be1 * ar_q1 + be1 * be1 * q1_q1
        ar_q2 = m2 + be1 * ar_q1
        q2_aq2 = m3 + 2.0 * be1 * q1_aar + be1 * be1 * q1_aq1
        a2 = rr2 / (m1 + be1 * r_q1)
        rr3 = a2 * a2 * q2_q2 - rr2
        be2 = rr3 / rr2
        a3 = rr3 / (m1 - 2.0 * a2 * ar_q2 + a2 * a2 * q2_aq2 - be2 * rr3 / a2)

        def update_row(row, unused):
            keep = keep_of(row)
            own_row = (row >= 1) & (row <= NODES_Y)
            for m in range(3):
                r2 = v0[m, row]
                ar2 = jnp.where(own_planes & own_row, v1[m, row], copy_rx[parity, m, row])
                ar2 = jnp.where(all_planes, keep * ar2, 0.0)
                aar2 = keep * assembled(
                    v2[m, row],
                    sum_rx[sum_parity, 0, m, row],
                    sum_rx[sum_parity, 1, m, row],
                    sum_rx[sum_parity, 2, m, row],
                    row,
                )
                old1, old0 = q1[m, row], q0[m, row]
                q2 = ar2 + be1 * old1
                aq1 = (old1 - be0 * old0 - ar2) * ia1
                r3 = r2 - a2 * q2
                q3 = ar2 - a2 * (aar2 + be1 * aq1) + be2 * q2
                d2 = r2 + be1 * d1[m, row]
                d3 = r3 + be2 * d2
                x[m, row] = x[m, row] + (a2 * d2 + a3 * d3)
                v0[m, row] = r3 - a3 * q3
                q1[m, row] = q3
                q0[m, row] = q2
                d1[m, row] = d3
            return unused

        lax.fori_loop(0, ROWS, update_row, 0)
        pltpu.make_async_copy(rest, rest, all_send.at[parity]).wait()
        return be2, 1.0 / a3, 1.0 / a2, rr3

    none = jnp.zeros((1, 1), F32)
    lax.fori_loop(0, OUTER, outer, (none, none, none, none + 1.0))

    stores = []
    for i in range(NODES_X):
        stores.append(pltpu.make_async_copy(x.at[:, 1:18, i + 1], increment_hbm.at[:, i], out_sem.at[0, i]))
        stores.append(pltpu.make_async_copy(v0.at[:, 1:18, i + 1], residual_hbm.at[:, i], out_sem.at[1, i]))
    for copy in stores:
        copy.start()
    for copy in stores:
        copy.wait()


def solution(mesh):
    size_x, size_y = mesh.shape["gx"], mesh.shape["gy"]
    peers = size_x * size_y
    field = jax.ShapeDtypeStruct((3, NODES_X, NODES_Y, NZ), F32)

    def vmem(*shape, dtype=F32):
        return pltpu.VMEM(shape, dtype)

    def node(*lead):
        return vmem(*lead, ROWS, SUB, NZ)

    dma = pltpu.SemaphoreType.DMA
    scratch = [
        node(3), node(3), node(), node(), node(3), vmem(BY, SUB, NZ), vmem(HIDDEN_LAYERS, HID, HID),
        vmem(6, BY, SUB, NZ), vmem(NZ, SLOTS, dtype=BF16), vmem(SLOTS, NZ, dtype=BF16),
        vmem(COLUMNS, SLOTS, dtype=BF16), vmem(BY * SUB, SLOTS), vmem(SLOTS, 128, dtype=BF16),
        vmem(128, SLOTS), vmem(32, SLOTS), vmem(2 * GROUP * COLUMNS, SLOTS, dtype=BF16),
        vmem(N_SCATTER, BY, SUB, NZ),
        vmem(N_PAIRS, BY, SUB, NZ), vmem(N_PAIRS, BY + 2, SUB, NZ), vmem(N_PAIRS, BY + 2, SUB, NZ),
        node(3), node(3), node(3), node(3), node(3), node(3), node(3),
        node(2, 3, 3), node(2, 3), vmem(2, peers, 1, 128),
        dma((5, 5)), dma((2, 5)), dma((8,)), dma((8,)), dma((8,)), dma((8,)),
        dma((2, 8)), dma((2, 8)), dma((2, 8)), dma((2, 8)), dma((2,)), dma((2,)),
    ]

    def body(u_now, load, mass, modulus, plastic_ids, plastic_count, w_in, w_hidden, w_head):
        hbm = pl.BlockSpec(memory_space=pl.ANY)
        local = pl.BlockSpec(memory_space=pltpu.VMEM)
        return pl.pallas_call(
            lambda *refs: kernel(size_x, size_y, *refs),
            out_shape=(field, field),
            in_specs=[
                hbm, hbm, hbm, hbm, local, pl.BlockSpec(memory_space=pltpu.SMEM), local, hbm, local,
            ],
            out_specs=(hbm, hbm),
            scratch_shapes=scratch,
            compiler_params=pltpu.CompilerParams(
                collective_id=0, has_side_effects=True, vmem_limit_bytes=60 * 2**20
            ),
        )(u_now, load, mass, modulus, plastic_ids.reshape(1, SLOTS), plastic_count, w_in, w_hidden, w_head)

    split_field = P(None, "gx", "gy", None)
    split_block = P("gx", "gy", None)
    return jax.shard_map(
        body,
        mesh=mesh,
        in_specs=(
            split_field, split_field, split_block, split_block, split_block, P("gx", "gy"), P(), P(), P(),
        ),
        out_specs=(split_field, split_field),
        check_vma=False,
    )
```

time: 1610 us -> 92.2 us (0.06); the launches traced: 1590 us -> 91.9 us
  blocking collectives: 726 us -> 0 us
  local copies, waits for them, and re-layouts: 462 us -> 8.98 us
  other arithmetic: 187 us -> 0 us
  Pallas kernels: 0 us -> 81.6 us
  matrix products: 77.4 us -> 0 us
  starting transfers between devices: 60.6 us -> 0 us
  waiting for transfers between devices: 59.7 us -> 0 us
  between operations: 20.2 us -> 1.29 us
    psum x11 -> x0, blocking collectives: 726 us -> none  [the longest x6 393 us: squared_norm(): return lax.psum(inner(values, values), ('gx', 'gy'))]
    another operation x64 -> x0, local copies, waits for them, and re-layouts: 280 us -> none  [the longest x63 280 us: strain_of(): return jnp.stack(parts).reshape(6, -1)]
    gather x22 -> x0, local copies, waits for them, and re-layouts: 99.8 us -> none  [the longest x14 46.8 us: stress_of(): jnp.take(base, element_ids, axis=1)]
    scatter-add x14 -> x0, other arithmetic: 86.2 us -> none  [the longest x7 86.1 us: stress_of(): return base.at[:, element_ids].add(change)]
    pallas_call x0 -> x1, Pallas kernels: none -> 81.6 us  [body(): pl.pallas_call(lambda *refs: kernel(size_x, size_y, *refs), out_shape=(fi...]
    dot_general x18 -> x0, matrix products: 77.4 us -> none  [the longest x6 52.6 us: body(): jnp.einsum('ijp,jp->ip', tangent, jnp.take(apply_strain, element_ids, axi...]
    mul x107 -> x0, other arithmetic: 66 us -> none  [the longest x7 55.3 us: elastic_stress(): return moduli[None] * jnp.concatenate([normal, shear], 0)]
    ppermute x28 -> x0, starting transfers between devices: 60.6 us -> none  [the longest x14 38.1 us: with_halo(): lax.ppermute(tail, axis, [(i, (i + 1) % count) for i in range(ends)])]
  transfers between devices with their start and end apart: 28 -> 0, of which waited for: 20 -> 0; matrix products, arithmetic and copies ran while one was open for 1% -> 0% of each run, Pallas kernels for 0% -> 0%
where the time goes in v1:
time: 92.2 us; the launch traced here: 91.9 us
  Pallas kernels  81.6 us (89%)
  local copies, waits for them, and re-layouts  8.98 us (10%)
  between operations  1.29 us (1%)
    pallas_call x1, Pallas kernels, body(): pl.pallas_call(lambda *refs: kernel(size_x, size_y, *refs), out_shape=(fi...  81.6 us
    unnamed x3, local copies, waits for them, and re-layouts  5.28 us
    pallas_call x2, local copies, waits for them, and re-layouts, body(): pl.pallas_call(lambda *refs: kernel(size_x, size_y, *refs), out_shape=(fi...  3.71 us

profile of v1, /device:TPU:1, one launch (start us, length us, event | category | flops | bytes accessed | tf_op | source)
XLA Modules:
  0.0 91.9 jit_solution(5020114418524244344)
XLA Ops:
  1.3 1.7 %copy.13.refs_8_ = f32[512,42]{1,0:T(8,128)} copy(f32[512,42]{0,1:T(8,128)} %param.17) | data formatting | bytes 172032 | tf_op args[8]
  3.0 1.8 %copy.11.refs_0_ = f32[3,5,17,256]{3,2,1,0:T(8,128)} copy(f32[3,5,17,256]{3,0,2,1:T(4,128)} %param.9) | data formatting | bytes 522240 | tf_op args[0]
  4.8 1.8 %copy.12.refs_1_ = f32[3,5,17,256]{3,2,1,0:T(8,128)} copy(f32[3,5,17,256]{3,0,2,1:T(4,128)} %param.10) | data formatting | bytes 522240 | tf_op args[1]
  6.6 81.6 %shard_map.104 = (f32[3,5,17,256]{3,2,1,0:T(8,128)}, f32[3,5,17,256]{3,2,1,0:T(8,128)}) custom-call(f32[3,5,17,256]{3,2,1,0:T(8,128)} %copy.11.refs_0_, f32[3,5,17,256]{3,2,1,0:T(8,128)} %copy.12.refs_1_, f32[5,17,256]{2,1,0:T(8,128)} %refs_2_.1, f32[4,16,256]{2,1,0:T(8,128)} %refs_3_.1, s32[1,1024]{1,0:T(1,128)} %bitcast.1, s32[1,1]{1,0:T(1,128)S(6)} %copy.16.refs_5_, ...), custom_call_target="tpu_custom_call" | custom-call | tf_op jit(solution)/shard_map/pallas_call | solution.py:593
  88.2 1.9 %copy.14 = f32[3,5,17,256]{3,0,2,1:T(4,128)} copy(f32[3,5,17,256]{3,2,1,0:T(8,128)} %get-tuple-element.2) | data formatting | bytes 522240 | tf_op jit(solution)/shard_map/pallas_call | solution.py:593
  90.0 1.9 %copy.15 = f32[3,5,17,256]{3,0,2,1:T(4,128)} copy(f32[3,5,17,256]{3,2,1,0:T(8,128)} %get-tuple-element.3) | data formatting | bytes 522240 | tf_op jit(solution)/shard_map/pallas_call | solution.py:593

commit v2 on v1

v2 whole, which is shorter than its diff:
```python
import jax
import jax.numpy as jnp
from jax import lax
from jax.experimental import pallas as pl
from jax.experimental.pallas import tpu as pltpu
from jax.sharding import PartitionSpec as P

MESH = pl.DeviceIdType.MESH
F32, BF16 = jnp.float32, jnp.bfloat16
LAME_FIRST = 0.3 / (1.3 * 0.4)
LAME_SECOND = 1.0 / 2.6

BX, BY, NZ = 4, 16, 256
NODES_X, NODES_Y = BX + 1, BY + 1
ROWS = BY + 3
SUB = 8
SLOTS, HID, HIDDEN_LAYERS = 1024, 512, 3
COLUMNS = BY * BX
OUTER = 3
GROUP = 7
RINGS = 4

PAIRS = [(a, b) for a in range(6) for b in range(a, 6)]
PAIR_OF = {}
for _at, (_a, _b) in enumerate(PAIRS):
    PAIR_OF[_a, _b] = PAIR_OF[_b, _a] = _at
N_PAIRS = len(PAIRS)
N_SCATTER = 28
LIVE, FIRST_PAIR = 6, 7

DIRECTIONS = [(dx, dy) for dx in (-1, 0, 1) for dy in (-1, 0, 1) if (dx, dy) != (0, 0)]


def iso(a, b):
    if a < 3 and b < 3:
        return LAME_FIRST + (2.0 * LAME_SECOND if a == b else 0.0)
    return LAME_SECOND if a == b else 0.0


def z_next(values):
    lane = lax.broadcasted_iota(jnp.int32, values.shape, 1)
    return jnp.where(lane == NZ - 1, 0.0, pltpu.roll(values, NZ - 1, 1))


def z_prev(values):
    lane = lax.broadcasted_iota(jnp.int32, values.shape, 1)
    return jnp.where(lane == 0, 0.0, pltpu.roll(values, 1, 1))


def x_pairs(values):
    upper = pltpu.roll(values, SUB - 1, 0)
    return upper + values, upper - values


def strain_row(low, high):
    a = [low[m][1] + high[m][1] for m in range(3)]
    b = [high[m][0] - low[m][0] for m in range(3)]
    c = [high[m][0] + low[m][0] for m in range(3)]
    yz, xz, xy = c[1] + b[2], c[0] + a[2], b[0] + a[1]
    return [
        z_next(a[0]) + a[0],
        z_next(b[1]) + b[1],
        z_next(c[2]) - c[2],
        z_next(yz) + (b[2] - c[1]),
        z_next(xz) + (a[2] - c[0]),
        z_next(xy) + xy,
    ]


def force_parts(stress):
    before = [z_prev(s) for s in stress]
    total = {n: stress[n] + before[n] for n in (0, 1, 3, 4, 5)}
    differ = {n: before[n] - stress[n] for n in (2, 3, 4)}
    parts = []
    for along_x, along_y, along_z in ((0, 5, 4), (5, 1, 3), (4, 3, 2)):
        parts.append(
            (
                total[along_x],
                differ[along_z] - total[along_y],
                differ[along_z] + total[along_y],
            )
        )
    return parts


def force_of(along_x, other):
    return pltpu.roll(along_x + other, 1, 0) + (other - along_x)


def split(values):
    high = values.astype(BF16)
    return high, (values - high.astype(F32)).astype(BF16)


def mm(a, b):
    return jnp.dot(a, b, preferred_element_type=F32)


def face(dx, dy, depth):
    if depth == 2:
        sx = {-1: slice(1, 3), 0: slice(1, 6), 1: slice(4, 6)}[dx]
        tx = {-1: slice(5, 7), 0: slice(1, 6), 1: slice(0, 2)}[dx]
        sy = {-1: slice(1, 3), 0: slice(1, 18), 1: slice(16, 18)}[dy]
        ty = {-1: slice(17, 19), 0: slice(1, 18), 1: slice(0, 2)}[dy]
    else:
        sx = {-1: slice(2, 3), 0: slice(1, 6), 1: slice(4, 5)}[dx]
        tx = {-1: slice(6, 7), 0: slice(1, 6), 1: slice(0, 1)}[dx]
        sy = {-1: slice(2, 3), 0: slice(1, 18), 1: slice(16, 17)}[dy]
        ty = {-1: slice(18, 19), 0: slice(1, 18), 1: slice(0, 1)}[dy]
    return sy, sx, ty, tx


def element_face(dx, dy):
    sx = {-1: slice(1, 2), 0: slice(1, 5), 1: slice(4, 5)}[dx]
    tx = {-1: slice(5, 6), 0: slice(1, 5), 1: slice(0, 1)}[dx]
    sy = {-1: slice(1, 2), 0: slice(1, 17), 1: slice(16, 17)}[dy]
    ty = {-1: slice(17, 18), 0: slice(1, 17), 1: slice(0, 1)}[dy]
    return sy, sx, ty, tx


def all_offsets(size_x, size_y):
    offsets = [
        (z, core, x, y)
        for z in range(size_x // 2)
        for core in range(2)
        for x in range(size_y // RINGS)
        for y in range(RINGS)
    ][1:]

    def hops(offset):
        z, core, x, y = offset
        return sum(min(d, RINGS - d) for d in (z, x, y)) * 2 + core

    return sorted(offsets, key=hops, reverse=True)


def by_rows(first, last, width, body, carry):
    assert (last - first) % width == 0

    def block(at, carry):
        for n in range(width):
            carry = body(first + at * width + n, carry)
        return carry

    return lax.fori_loop(0, (last - first) // width, block, carry)


def kernel(
    size_x, size_y,
    u_hbm, load_hbm, mass_hbm, modulus_hbm, ids_ref, count_ref, w_in_ref, w_hidden_hbm, w_head_ref,
    increment_hbm, residual_hbm,
    ux, lx, mass_part, mass_full, mass_rx, modulus, weights,
    strain_now, onehot_k, onehot_kt, onehot_r, onehot_r8, inputs_t, out_t, values, lhs, scattered,
    tangent,
    v0, v1, v2, q1, q0, d1, x, sum_rx, copy_rx, gathered,
    load_sem, out_sem, mass_send, mass_recv, tan_send, tan_recv,
    sum_send, sum_recv, copy_send, copy_recv, all_send, all_recv,
):
    index_x, index_y = lax.axis_index("gx"), lax.axis_index("gy")
    me = index_x * size_y + index_y
    peers = size_x * size_y
    neighbours = [
        (lax.rem(index_x + dx + size_x, size_x), lax.rem(index_y + dy + size_y, size_y))
        for dx, dy in DIRECTIONS
    ]

    ring_x, ring_y = index_y // RINGS, lax.rem(index_y, RINGS)
    ring_z, core = index_x // 2, lax.rem(index_x, 2)
    at_z = [lax.rem(ring_z + d, RINGS) * 2 for d in range(size_x // 2)]
    at_core = [core, 1 - core]
    at_ring_x = [lax.rem(ring_x + d, RINGS) * RINGS for d in range(size_y // RINGS)]
    at_ring_y = [lax.rem(ring_y + d, RINGS) for d in range(RINGS)]
    along_gx = [[z + c for c in at_core] for z in at_z]
    along_gy = [[a + b for b in at_ring_y] for a in at_ring_x]
    others = [
        (along_gx[z][c], along_gy[a][b]) for z, c, a, b in all_offsets(size_x, size_y)
    ]

    for ref in (mass_part, modulus):
        ref[...] = jnp.zeros_like(ref)
    u_loads, modulus_loads, mass_loads, load_loads, weight_loads = [], [], [], [], []
    for i in range(NODES_X):
        for m in range(3):
            u_loads.append(pltpu.make_async_copy(u_hbm.at[i, :, m : m + 1], ux.at[m, 1:18, i + 1 : i + 2], load_sem.at[m, i]))
    for layer in range(HIDDEN_LAYERS):
        weight_loads.append(pltpu.make_async_copy(w_hidden_hbm.at[layer], weights.at[layer], load_sem.at[8, layer]))
    for i in range(BX):
        modulus_loads.append(pltpu.make_async_copy(modulus_hbm.at[i], modulus.at[:, i + 1], load_sem.at[6, i]))
    for i in range(NODES_X):
        mass_loads.append(pltpu.make_async_copy(mass_hbm.at[i], mass_part.at[1:18, i + 1], load_sem.at[7, i]))
        for m in range(3):
            load_loads.append(pltpu.make_async_copy(load_hbm.at[i, :, m : m + 1], lx.at[m, 1:18, i + 1 : i + 2], load_sem.at[3 + m, i]))
    loads = u_loads + weight_loads + modulus_loads + mass_loads + load_loads
    for copy in loads:
        copy.start()

    tangent[...] = jnp.zeros_like(tangent)
    barrier = pltpu.get_barrier_semaphore()
    for device in others:
        pl.semaphore_signal(barrier, inc=1, device_id=device, device_id_type=MESH)
    for ref in (q1, q0, d1, x):
        ref[...] = jnp.zeros_like(ref)

    ids = ids_ref[...]
    slot = lax.broadcasted_iota(jnp.int32, (1, SLOTS), 1)
    live = jnp.where(slot < count_ref[0, 0], 1.0, 0.0)
    at_k = ids & (NZ - 1)
    at_j = (ids >> 8) & (BY - 1)
    at_i = ids >> 12
    onehot_k[...] = jnp.where(
        lax.broadcasted_iota(jnp.int32, (NZ, SLOTS), 0) == at_k, 1.0, 0.0
    ).astype(BF16)
    onehot_r[...] = jnp.where(
        lax.broadcasted_iota(jnp.int32, (COLUMNS, SLOTS), 0) == at_j * BX + at_i, live, 0.0
    ).astype(BF16)
    onehot_r8[...] = jnp.where(
        lax.broadcasted_iota(jnp.int32, (BY * SUB, SLOTS), 0) == at_j * SUB + at_i + 1, 1.0, 0.0
    )
    k_column = jnp.broadcast_to(at_k.astype(F32), (128, SLOTS)).T
    lane_k = lax.broadcasted_iota(jnp.int32, (SLOTS, 128), 1).astype(F32)
    onehot_kt[:, 0:128] = jnp.where(k_column == lane_k, 1.0, 0.0).astype(BF16)
    onehot_kt[:, 128:256] = jnp.where(k_column == lane_k + 128.0, 1.0, 0.0).astype(BF16)

    sub = lax.broadcasted_iota(jnp.int32, (SUB, NZ), 0)
    own_elements = (sub >= 1) & (sub <= BX)
    for copy in u_loads:
        copy.wait()

    def pairs_of(ref, row):
        return [x_pairs(ref[m, row]) for m in range(3)]

    def strain_step(row, low):
        high = pairs_of(ux, row + 1)
        for n, value in enumerate(strain_row(low, high)):
            strain_now[n, row - 1] = jnp.where(own_elements, 0.25 * value, 0.0)
        return high

    by_rows(1, 1 + BY, 8, strain_step, pairs_of(ux, 1))

    picked = []
    for n in range(6):
        high, low = split(strain_now[n].reshape(BY * SUB, NZ))
        rows = mm(high, onehot_k[...]) + mm(low, onehot_k[...])
        picked.append(jnp.sum(rows * onehot_r8[...], axis=0, keepdims=True))
    eps = jnp.concatenate(picked + [jnp.zeros((2, SLOTS), F32)], axis=0)
    eps_high = eps.astype(BF16).astype(F32)
    stacked = jnp.concatenate(
        [eps_high, eps - eps_high, eps_high, jnp.zeros((104, SLOTS), F32)], axis=0
    )
    inputs_t[...] = stacked.T.astype(BF16)

    w_in = jnp.concatenate([w_in_ref[...], jnp.zeros((2, HID), F32)], axis=0)
    w_in_high = w_in.astype(BF16).astype(F32)
    w_first = jnp.concatenate(
        [w_in_high, w_in_high, w_in - w_in_high, jnp.zeros((104, HID), F32)], axis=0
    ).astype(BF16)
    to_row = lax.broadcasted_iota(jnp.int32, (128, 42), 0)
    from_out = lax.broadcasted_iota(jnp.int32, (128, 42), 1)
    place = jnp.where(
        (from_out == (to_row // 8) * 6 + to_row % 8) & (to_row % 8 < 6) & (to_row < 56), 1.0, 0.0
    ).astype(BF16)
    head_high, head_low = split(w_head_ref[...])
    head_high = mm(place, head_high).T.astype(BF16)
    head_low = mm(place, head_low).T.astype(BF16)
    for copy in weight_loads:
        copy.wait()
    halves = [split(weights[layer]) for layer in range(HIDDEN_LAYERS)]

    def product(hidden, parts):
        high, low = split(hidden)
        return mm(high, parts[0]) + (mm(low, parts[0]) + mm(high, parts[1]))

    half = SLOTS // 2
    left, right = mm(inputs_t[0:half], w_first), mm(inputs_t[half:SLOTS], w_first)
    for parts in halves + [(head_high, head_low)]:
        left = product(jnp.tanh(left), parts)
        right = product(jnp.tanh(right), parts)
    out_t[:, 0:half] = left.T
    out_t[:, half:SLOTS] = right.T

    for copy in mass_loads:
        copy.wait()
    pl.semaphore_wait(barrier, peers - 1)
    mass_copies = []
    for q, ((dx, dy), device) in enumerate(zip(DIRECTIONS, neighbours)):
        sy, sx, ty, tx = face(dx, dy, 2)
        kind = 0 if dy == 0 else (1 if dx == 0 else 2)
        copy = pltpu.make_async_remote_copy(
            mass_part.at[sy, sx], mass_rx.at[kind, ty, tx], mass_send.at[q], mass_recv.at[q],
            device_id=device, device_id_type=MESH,
        )
        copy.start()
        mass_copies.append(copy)

    values[0:6] = out_t[0:6]
    values[LIVE : LIVE + 1] = jnp.ones((1, SLOTS), F32)
    factor = [out_t[8 * (a + 1) : 8 * (a + 2)] for a in range(6)]
    for at, (a, b) in enumerate(PAIRS):
        values[FIRST_PAIR + at : FIRST_PAIR + at + 1] = jnp.sum(
            factor[a] * factor[b], axis=0, keepdims=True
        ) * (1.0 / 6.0)

    def scatter_group(at):
        for n in range(GROUP):
            high, low = split(values[at * GROUP + n : at * GROUP + n + 1])
            rows = onehot_r[...]
            lhs[n * COLUMNS : (n + 1) * COLUMNS] = rows * high
            lhs[(GROUP + n) * COLUMNS : (GROUP + n + 1) * COLUMNS] = rows * low
        spread = mm(lhs[...], onehot_kt[...])
        spread = spread[: GROUP * COLUMNS] + spread[GROUP * COLUMNS :]
        for n in range(GROUP):
            for g in range(BY // 2):
                start = n * COLUMNS + g * SUB
                both = spread[start : start + SUB]
                scattered[at * GROUP + n, 2 * g] = jnp.where(own_elements, pltpu.roll(both, 1, 0), 0.0)
                scattered[at * GROUP + n, 2 * g + 1] = jnp.where(own_elements, pltpu.roll(both, 5, 0), 0.0)

    def sum_copies(parity):
        copies = []
        for q, ((dx, dy), device) in enumerate(zip(DIRECTIONS, neighbours)):
            sy, sx, ty, tx = face(dx, dy, 2)
            kind = 0 if dy == 0 else (1 if dx == 0 else 2)
            copies.append(
                pltpu.make_async_remote_copy(
                    v2.at[:, sy, sx], sum_rx.at[parity, kind, :, ty, tx],
                    sum_send.at[parity, q], sum_recv.at[parity, q],
                    device_id=device, device_id_type=MESH,
                )
            )
        return copies

    def exact_copies(parity):
        copies = []
        for q, ((dx, dy), device) in enumerate(zip(DIRECTIONS, neighbours)):
            sy, sx, ty, tx = face(dx, dy, 1)
            copies.append(
                pltpu.make_async_remote_copy(
                    v1.at[:, sy, sx], copy_rx.at[parity, :, ty, tx],
                    copy_send.at[parity, q], copy_recv.at[parity, q],
                    device_id=device, device_id_type=MESH,
                )
            )
        return copies

    global_x = index_x * BX + sub - 1
    keep_x = jnp.where(
        (global_x >= 0) & (global_x < size_x * BX) & (sub < SUB - 1), 1.0, 0.0
    )
    own_planes = (sub >= 1) & (sub <= NODES_X)
    rim_planes = ((sub <= 1) & (index_x > 0)) | ((sub >= NODES_X) & (sub <= NODES_X + 1))
    halo_planes = (sub == 0) | (sub == NODES_X + 1)
    flank_low, corner_low = own_planes & (index_y > 0), rim_planes & (index_y > 0)
    valid_elements = (sub <= BX + 1) & ((sub >= 1) | (index_x > 0))

    def keep_of(row):
        global_y = index_y * BY + row - 1
        inside = jnp.where((global_y >= 0) & (global_y < size_y * BY), 1.0, 0.0)
        return keep_x * inside

    def assembled(part, received, row):
        at_rim = isinstance(row, int)
        total = jnp.zeros((SUB, NZ), F32)
        if not at_rim or 1 <= row <= NODES_Y:
            total = part + jnp.where(rim_planes, received(0), 0.0)
        if at_rim:
            flank, corner = (flank_low, corner_low) if row <= 1 else (own_planes, rim_planes)
            total = total + jnp.where(flank, received(1), 0.0) + jnp.where(corner, received(2), 0.0)
        return total

    def all_rows(body):
        for row in (0, 1, NODES_Y, NODES_Y + 1):
            body(row)

        def inner(row, carry):
            body(row)
            return carry

        by_rows(2, NODES_Y, 5, inner, 0)

    def stress_now(row):
        scale = 0.25 * modulus[row]
        base = scale * (1.0 - 0.75 * scattered[LIVE, row])
        eps_row = [strain_now[n, row] for n in range(6)]
        trace = LAME_FIRST * (eps_row[0] + eps_row[1] + eps_row[2])
        elastic = [trace + 2.0 * LAME_SECOND * eps_row[n] for n in range(3)]
        elastic += [LAME_SECOND * eps_row[n] for n in range(3, 6)]
        return [base * elastic[n] + scale * scattered[n, row] for n in range(6)]

    zero = jnp.zeros((SUB, NZ), F32)
    no_parts = [(zero, zero)] * 3

    def residual_step(row, before):
        parts = force_parts(stress_now(row - 1))
        for m in range(3):
            force = force_of(parts[m][0] + before[m][0], parts[m][1] + before[m][1])
            v2[m, row] = jnp.where(own_planes, lx[m, row] - force, 0.0)
        return [(parts[m][0], parts[m][2]) for m in range(3)]

    scatter_group(0)
    for copy in modulus_loads + load_loads:
        copy.wait()
    last = by_rows(1, 1 + BY, 8, residual_step, no_parts)
    for m in range(3):
        v2[m, NODES_Y] = jnp.where(own_planes, lx[m, NODES_Y] - force_of(*last[m]), 0.0)

    first_copies = sum_copies(0)
    for copy in first_copies:
        copy.start()

    tangent_copies = []
    for group in range(N_PAIRS // GROUP):
        scatter_group(group + 1)

        def tangent_row(row, carry):
            scale = modulus[row] * (1.0 / 16.0)
            base = scale * (1.0 - 0.75 * scattered[LIVE, row])
            for at in range(group * GROUP, (group + 1) * GROUP):
                entry = scale * scattered[FIRST_PAIR + at, row]
                if iso(*PAIRS[at]):
                    entry = entry + base * iso(*PAIRS[at])
                tangent[at, row + 1, 1 : 1 + BX] = entry[1 : 1 + BX]
            return carry

        by_rows(0, BY, 4, tangent_row, 0)
        entries = pl.ds(group * GROUP, GROUP)
        for q, ((dx, dy), device) in enumerate(zip(DIRECTIONS, neighbours)):
            sy, sx, ty, tx = element_face(dx, dy)
            copy = pltpu.make_async_remote_copy(
                tangent.at[entries, sy, sx], tangent.at[entries, ty, tx],
                tan_send.at[group, q], tan_recv.at[group, q],
                device_id=device, device_id_type=MESH,
            )
            copy.start()
            tangent_copies.append(copy)

    for copy in mass_copies:
        copy.wait()

    def mass_row(row):
        mass_full[row] = assembled(mass_part[row], lambda kind: mass_rx[kind, row], row)

    all_rows(mass_row)
    for copy in first_copies:
        copy.wait()

    def start_row(row):
        keep = keep_of(row)
        for m in range(3):
            part = None if isinstance(row, int) and row in (0, NODES_Y + 1) else v2[m, row]
            v0[m, row] = keep * assembled(part, lambda kind: sum_rx[0, kind, m, row], row)

    all_rows(start_row)
    for copy in tangent_copies:
        copy.wait()

    def stress_row(row, strain):
        entries = [tangent[at, row] for at in range(N_PAIRS)]
        result = []
        for a in range(6):
            total = entries[PAIR_OF[a, 0]] * strain[0]
            for b in range(1, 6):
                total = total + entries[PAIR_OF[a, b]] * strain[b]
            result.append(total)
        return result

    def first_image(row, carry):
        low, before = carry
        high = pairs_of(v0, row + 1)
        present = valid_elements & (row + index_y > 0)
        strain = [jnp.where(present, value, 0.0) for value in strain_row(low, high)]
        parts = force_parts(stress_row(row, strain))
        keep = keep_of(row)
        for m in range(3):
            force = force_of(parts[m][0] + before[m][0], parts[m][1] + before[m][1])
            v1[m, row] = keep * (force + mass_full[row] * v0[m, row])
        return high, [(parts[m][0], parts[m][2]) for m in range(3)]

    def second_image(row, carry):
        low, before, sums = carry
        high = pairs_of(v1, row + 1)
        strain = [jnp.where(own_elements, value, 0.0) for value in strain_row(low, high)]
        parts = force_parts(stress_row(row, strain))
        rr, r_ar, ar_ar, ar_aar = sums
        for m in range(3):
            here, image = v0[m, row], v1[m, row]
            force = force_of(parts[m][0] + before[m][0], parts[m][1] + before[m][1])
            force = force + mass_part[row] * image
            v2[m, row] = force
            rr = rr + here * here
            r_ar = r_ar + here * image
            ar_ar = ar_ar + image * image
            ar_aar = ar_aar + image * force
        return high, [(parts[m][0], parts[m][2]) for m in range(3)], (rr, r_ar, ar_ar, ar_aar)

    lane = lax.broadcasted_iota(jnp.int32, (1, 128), 1)

    def outer(step, carry):
        be0, ia1, ia0, rr_before = carry
        parity = lax.rem(step, 2)
        sum_parity = lax.rem(step + 1, 2)
        by_rows(0, BY + 2, 6, first_image, (pairs_of(v0, 0), no_parts))
        exact = exact_copies(parity)
        for copy in exact:
            copy.start()
        _, before, sums = by_rows(
            1, 1 + BY, 8, second_image, (pairs_of(v1, 1), no_parts, (zero,) * 4)
        )
        ar_aar = sums[3]
        for m in range(3):
            image = v1[m, NODES_Y]
            force = force_of(*before[m]) + mass_part[NODES_Y] * image
            v2[m, NODES_Y] = force
            ar_aar = ar_aar + jnp.where(own_planes, image * force, 0.0)
        summed = sum_copies(sum_parity)
        for copy in summed:
            copy.start()

        message = jnp.zeros((1, 128), F32)
        for at, (value, mask) in enumerate(
            ((sums[0], own_elements), (sums[1], own_elements), (sums[2], own_elements), (ar_aar, own_planes))
        ):
            total = jnp.sum(jnp.where(mask, value, 0.0), axis=0, keepdims=True)
            total = jnp.sum(total, axis=1, keepdims=True)
            message = message + jnp.where(lane == at, total, 0.0)
        gathered[parity, me] = message

        for device in others:
            pltpu.make_async_remote_copy(
                gathered.at[parity, me], gathered.at[parity, me],
                all_send.at[parity], all_recv.at[parity],
                device_id=device, device_id_type=MESH,
            ).start()
        for copy in exact + summed:
            copy.wait()

        def image_row(row):
            keep = keep_of(row)
            outside = isinstance(row, int) and row in (0, NODES_Y + 1)
            for m in range(3):
                rim = copy_rx[parity, m, row]
                if outside:
                    ar2 = jnp.where(sub <= NODES_X + 1, rim, 0.0)
                else:
                    ar2 = jnp.where(halo_planes, rim, v1[m, row])
                ar2 = keep * ar2
                part = None if outside else v2[m, row]
                v2[m, row] = keep * assembled(part, lambda kind: sum_rx[sum_parity, kind, m, row], row)
                v1[m, row] = ar2
                q0[m, row] = (q1[m, row] - be0 * q0[m, row] - ar2) * ia1

        all_rows(image_row)
        rest = gathered.at[parity, 0 : peers - 1]
        pltpu.make_async_copy(rest, rest, all_recv.at[parity]).wait()
        totals = jnp.sum(gathered[parity], axis=0)
        rr2, m1, m2, m3 = [
            jnp.sum(jnp.where(lane == at, totals, 0.0), axis=1, keepdims=True) for at in range(4)
        ]
        be1 = jnp.where(step == 0, 0.0, rr2 / rr_before)
        r_q1 = -rr2 * ia1
        ar_q1 = (r_q1 - m1) * ia1
        q1_q1 = (rr_before + rr2) * ia1 * ia1
        ar_q0 = rr2 * ia1 * ia0
        q1_q0 = -rr_before * ia1 * ia0
        q1_aar = ia1 * (ar_q1 - be0 * ar_q0 - m2)
        q1_aq1 = ia1 * (q1_q1 - be0 * q1_q0 - ar_q1)
        q2_q2 = m2 + 2.0 * be1 * ar_q1 + be1 * be1 * q1_q1
        ar_q2 = m2 + be1 * ar_q1
        q2_aq2 = m3 + 2.0 * be1 * q1_aar + be1 * be1 * q1_aq1
        a2 = rr2 / (m1 + be1 * r_q1)
        rr3 = a2 * a2 * q2_q2 - rr2
        be2 = rr3 / rr2
        a3 = rr3 / (m1 - 2.0 * a2 * ar_q2 + a2 * a2 * q2_aq2 - be2 * rr3 / a2)

        def update_row(row, unused):
            for m in range(3):
                ar2, old = v1[m, row], q1[m, row]
                q2 = ar2 + be1 * old
                r3 = v0[m, row] - a2 * q2
                q3 = ar2 - a2 * (v2[m, row] + be1 * q0[m, row]) + be2 * q2
                d2 = v0[m, row] + be1 * d1[m, row]
                d3 = r3 + be2 * d2
                x[m, row] = x[m, row] + (a2 * d2 + a3 * d3)
                v0[m, row] = r3 - a3 * q3
                q1[m, row] = q3
                q0[m, row] = q2
                d1[m, row] = d3
            return unused

        by_rows(0, ROWS - 1, 6, update_row, 0)
        update_row(ROWS - 1, 0)
        pltpu.make_async_copy(rest, rest, all_send.at[parity]).wait()
        return be2, 1.0 / a3, 1.0 / a2, rr3

    none = jnp.zeros((1, 1), F32)
    lax.fori_loop(0, OUTER, outer, (none, none, none, none + 1.0))

    stores = []
    for i in range(NODES_X):
        for m in range(3):
            stores.append(pltpu.make_async_copy(x.at[m, 1:18, i + 1 : i + 2], increment_hbm.at[i, :, m : m + 1], out_sem.at[0, m, i]))
            stores.append(pltpu.make_async_copy(v0.at[m, 1:18, i + 1 : i + 2], residual_hbm.at[i, :, m : m + 1], out_sem.at[1, m, i]))
    for copy in stores:
        copy.start()
    for copy in stores:
        copy.wait()


def solution(mesh):
    size_x, size_y = mesh.shape["gx"], mesh.shape["gy"]
    peers = size_x * size_y
    field = jax.ShapeDtypeStruct((NODES_X, NODES_Y, 3, NZ), F32)

    def vmem(*shape, dtype=F32):
        return pltpu.VMEM(shape, dtype)

    def node(*lead):
        return vmem(*lead, ROWS, SUB, NZ)

    dma = pltpu.SemaphoreType.DMA
    scratch = [
        node(3), node(3), node(), node(), node(3), vmem(BY, SUB, NZ), vmem(HIDDEN_LAYERS, HID, HID),
        vmem(6, BY, SUB, NZ), vmem(NZ, SLOTS, dtype=BF16), vmem(SLOTS, NZ, dtype=BF16),
        vmem(COLUMNS, SLOTS, dtype=BF16), vmem(BY * SUB, SLOTS), vmem(SLOTS, 128, dtype=BF16),
        vmem(128, SLOTS), vmem(32, SLOTS), vmem(2 * GROUP * COLUMNS, SLOTS, dtype=BF16),
        vmem(N_SCATTER, BY, SUB, NZ),
        vmem(N_PAIRS, BY + 2, SUB, NZ),
        node(3), node(3), node(3), node(3), node(3), node(3), node(3),
        node(2, 3, 3), node(2, 3), vmem(2, peers, 1, 128),
        dma((9, 5)), dma((2, 3, 5)), dma((8,)), dma((8,)), dma((3, 8)), dma((3, 8)),
        dma((2, 8)), dma((2, 8)), dma((2, 8)), dma((2, 8)), dma((2,)), dma((2,)),
    ]

    def body(u_now, load, mass, modulus, plastic_ids, plastic_count, w_in, w_hidden, w_head):
        hbm = pl.BlockSpec(memory_space=pl.ANY)
        local = pl.BlockSpec(memory_space=pltpu.VMEM)
        increment, residual = pl.pallas_call(
            lambda *refs: kernel(size_x, size_y, *refs),
            out_shape=(field, field),
            in_specs=[
                hbm, hbm, hbm, hbm, local, pl.BlockSpec(memory_space=pltpu.SMEM), local, hbm, local,
            ],
            out_specs=(hbm, hbm),
            scratch_shapes=scratch,
            compiler_params=pltpu.CompilerParams(
                collective_id=0, has_side_effects=True, vmem_limit_bytes=60 * 2**20
            ),
        )(
            u_now.transpose(1, 2, 0, 3), load.transpose(1, 2, 0, 3), mass, modulus,
            plastic_ids.reshape(1, SLOTS), plastic_count, w_in, w_hidden, w_head.T,
        )
        return increment.transpose(2, 0, 1, 3), residual.transpose(2, 0, 1, 3)

    split_field = P(None, "gx", "gy", None)
    split_block = P("gx", "gy", None)
    return jax.shard_map(
        body,
        mesh=mesh,
        in_specs=(
            split_field, split_field, split_block, split_block, split_block, P("gx", "gy"), P(), P(), P(),
        ),
        out_specs=(split_field, split_field),
        check_vma=False,
    )
```

time: 92.2 us -> 61.6 us (0.67)
  Pallas kernels: 81.6 us -> 56.5 us
  local copies, waits for them, and re-layouts: 8.98 us -> 3.54 us
    pallas_call x1, Pallas kernels: 81.6 us -> 56.5 us  [body(): pl.pallas_call(lambda *refs: kernel(size_x, size_y, *refs), out_shape=(fi...]
    pallas_call x2 -> x0, local copies, waits for them, and re-layouts: 3.71 us -> none  [body(): pl.pallas_call(lambda *refs: kernel(size_x, size_y, *refs), out_shape=(fi...]
    unnamed x3 -> x2, local copies, waits for them, and re-layouts: 5.28 us -> 3.54 us
where the time goes in v2:
time: 61.6 us; the launch traced here: 61.4 us
  Pallas kernels  56.5 us (92%)
  local copies, waits for them, and re-layouts  3.54 us (6%)
  between operations  1.29 us (2%)
    pallas_call x1, Pallas kernels, body(): pl.pallas_call(lambda *refs: kernel(size_x, size_y, *refs), out_shape=(fi...  56.5 us
    unnamed x2, local copies, waits for them, and re-layouts  3.54 us

profile of v2, /device:TPU:1, one launch (start us, length us, event | category | flops | bytes accessed | tf_op | source)
XLA Modules:
  0.0 61.4 jit_solution(15404873444944327796)
XLA Ops:
  1.3 56.5 %shard_map.104 = (f32[5,17,3,256]{3,2,1,0:T(4,128)}, f32[5,17,3,256]{3,2,1,0:T(4,128)}) custom-call(f32[5,17,3,256]{3,2,1,0:T(4,128)} %bitcast.6, f32[5,17,3,256]{3,2,1,0:T(4,128)} %bitcast.7, f32[5,17,256]{2,1,0:T(8,128)} %refs_2_.1, f32[4,16,256]{2,1,0:T(8,128)} %refs_3_.1, s32[1,1024]{1,0:T(1,128)} %bitcast.11, s32[1,1]{1,0:T(1,128)S(6)} %copy.13.refs_5_, ...), custom_call_target="tpu_custom_call" | custom-call | tf_op jit(solution)/shard_map/pallas_call | solution.py:636
  57.8 1.8 %copy.14 = f32[3,5,17,256]{3,0,2,1:T(4,128)} copy(f32[3,5,17,256]{3,0,2,1:T(4,128)} %bitcast.9) | data formatting | bytes 522240
  59.6 1.8 %copy.15 = f32[3,5,17,256]{3,0,2,1:T(4,128)} copy(f32[3,5,17,256]{3,0,2,1:T(4,128)} %bitcast.8) | data formatting | bytes 522240

commit v3 on v2

--- a/solution.py
+++ b/solution.py
@@ -147,9 +147,9 @@
 
 def kernel(
     size_x, size_y,
-    u_hbm, load_hbm, mass_hbm, modulus_hbm, ids_ref, count_ref, w_in_ref, w_hidden_hbm, w_head_ref,
+    u_hbm, load_hbm, mass_hbm, modulus_hbm, ids_hbm, count_hbm, w_in_hbm, w_hidden_hbm, w_head_hbm,
     increment_hbm, residual_hbm,
-    ux, lx, mass_part, mass_full, mass_rx, modulus, weights,
+    ids_ref, count_ref, w_in_ref, w_head_ref, ux, lx, mass_part, mass_full, mass_rx, modulus, weights,
     strain_now, onehot_k, onehot_kt, onehot_r, onehot_r8, inputs_t, out_t, values, lhs, scattered,
     tangent,
     v0, v1, v2, q1, q0, d1, x, sum_rx, copy_rx, gathered,
@@ -178,6 +178,11 @@
 
     for ref in (mass_part, modulus):
         ref[...] = jnp.zeros_like(ref)
+    small = ((ids_hbm, ids_ref), (count_hbm, count_ref), (w_in_hbm, w_in_ref), (w_head_hbm, w_head_ref))
+    small_loads = [
+        pltpu.make_async_copy(source, target, load_sem.at[9, at])
+        for at, (source, target) in enumerate(small)
+    ]
     u_loads, modulus_loads, mass_loads, load_loads, weight_loads = [], [], [], [], []
     for i in range(NODES_X):
         for m in range(3):
@@ -190,20 +195,19 @@
         mass_loads.append(pltpu.make_async_copy(mass_hbm.at[i], mass_part.at[1:18, i + 1], load_sem.at[7, i]))
         for m in range(3):
             load_loads.append(pltpu.make_async_copy(load_hbm.at[i, :, m : m + 1], lx.at[m, 1:18, i + 1 : i + 2], load_sem.at[3 + m, i]))
-    loads = u_loads + weight_loads + modulus_loads + mass_loads + load_loads
+    loads = small_loads + u_loads + weight_loads + modulus_loads + mass_loads + load_loads
     for copy in loads:
         copy.start()
 
-    tangent[...] = jnp.zeros_like(tangent)
     barrier = pltpu.get_barrier_semaphore()
     for device in others:
         pl.semaphore_signal(barrier, inc=1, device_id=device, device_id_type=MESH)
-    for ref in (q1, q0, d1, x):
-        ref[...] = jnp.zeros_like(ref)
+    for copy in small_loads:
+        copy.wait()
 
     ids = ids_ref[...]
     slot = lax.broadcasted_iota(jnp.int32, (1, SLOTS), 1)
-    live = jnp.where(slot < count_ref[0, 0], 1.0, 0.0)
+    live = jnp.where(slot < count_ref[...], 1.0, 0.0)
     at_k = ids & (NZ - 1)
     at_j = (ids >> 8) & (BY - 1)
     at_i = ids >> 12
@@ -262,9 +266,10 @@
     head_high, head_low = split(w_head_ref[...])
     head_high = mm(place, head_high).T.astype(BF16)
     head_low = mm(place, head_low).T.astype(BF16)
-    for copy in weight_loads:
-        copy.wait()
-    halves = [split(weights[layer]) for layer in range(HIDDEN_LAYERS)]
+    halves = []
+    for layer in range(HIDDEN_LAYERS):
+        weight_loads[layer].wait()
+        halves.append(split(weights[layer]))
 
     def product(hidden, parts):
         high, low = split(hidden)
@@ -306,14 +311,15 @@
             rows = onehot_r[...]
             lhs[n * COLUMNS : (n + 1) * COLUMNS] = rows * high
             lhs[(GROUP + n) * COLUMNS : (GROUP + n + 1) * COLUMNS] = rows * low
-        spread = mm(lhs[...], onehot_kt[...])
-        spread = spread[: GROUP * COLUMNS] + spread[GROUP * COLUMNS :]
-        for n in range(GROUP):
-            for g in range(BY // 2):
-                start = n * COLUMNS + g * SUB
-                both = spread[start : start + SUB]
-                scattered[at * GROUP + n, 2 * g] = jnp.where(own_elements, pltpu.roll(both, 1, 0), 0.0)
-                scattered[at * GROUP + n, 2 * g + 1] = jnp.where(own_elements, pltpu.roll(both, 5, 0), 0.0)
+        if at == 0:
+            spread = mm(lhs[...], onehot_kt[...])
+            return spread[: GROUP * COLUMNS] + spread[GROUP * COLUMNS :]
+        return mm(lhs[: GROUP * COLUMNS], onehot_kt[...]) + mm(lhs[GROUP * COLUMNS :], onehot_kt[...])
+
+    def element_rows(spread, n, g):
+        start = n * COLUMNS + g * SUB
+        both = spread[start : start + SUB]
+        return pltpu.roll(both, 1, 0), pltpu.roll(both, 5, 0)
 
     def sum_copies(parity):
         copies = []
@@ -396,7 +402,11 @@
             v2[m, row] = jnp.where(own_planes, lx[m, row] - force, 0.0)
         return [(parts[m][0], parts[m][2]) for m in range(3)]
 
-    scatter_group(0)
+    spread = scatter_group(0)
+    for n in range(GROUP):
+        for g in range(BY // 2):
+            for odd, entry in enumerate(element_rows(spread, n, g)):
+                scattered[n, 2 * g + odd] = jnp.where(own_elements, entry, 0.0)
     for copy in modulus_loads + load_loads:
         copy.wait()
     last = by_rows(1, 1 + BY, 8, residual_step, no_parts)
@@ -408,20 +418,19 @@
         copy.start()
 
     tangent_copies = []
+    planes = slice(1, 1 + BX)
     for group in range(N_PAIRS // GROUP):
-        scatter_group(group + 1)
-
-        def tangent_row(row, carry):
-            scale = modulus[row] * (1.0 / 16.0)
-            base = scale * (1.0 - 0.75 * scattered[LIVE, row])
-            for at in range(group * GROUP, (group + 1) * GROUP):
-                entry = scale * scattered[FIRST_PAIR + at, row]
-                if iso(*PAIRS[at]):
-                    entry = entry + base * iso(*PAIRS[at])
-                tangent[at, row + 1, 1 : 1 + BX] = entry[1 : 1 + BX]
-            return carry
-
-        by_rows(0, BY, 4, tangent_row, 0)
+        spread = scatter_group(group + 1)
+        for g in range(BY // 2):
+            scales = [modulus[2 * g + odd] * (1.0 / 16.0) for odd in range(2)]
+            bases = [scales[odd] * (1.0 - 0.75 * scattered[LIVE, 2 * g + odd]) for odd in range(2)]
+            for n in range(GROUP):
+                at = group * GROUP + n
+                for odd, entry in enumerate(element_rows(spread, n, g)):
+                    entry = scales[odd] * entry
+                    if iso(*PAIRS[at]):
+                        entry = entry + bases[odd] * iso(*PAIRS[at])
+                    tangent[at, 2 * g + odd + 1, planes] = entry[planes]
         entries = pl.ds(group * GROUP, GROUP)
         for q, ((dx, dy), device) in enumerate(zip(DIRECTIONS, neighbours)):
             sy, sx, ty, tx = element_face(dx, dy)
@@ -433,6 +442,8 @@
             copy.start()
             tangent_copies.append(copy)
 
+    for ref in (q1, q0, d1, x):
+        ref[...] = jnp.zeros_like(ref)
     for copy in mass_copies:
         copy.wait()
 
@@ -453,22 +464,21 @@
     for copy in tangent_copies:
         copy.wait()
 
-    def stress_row(row, strain):
+    def stress_row(row, strain, present):
         entries = [tangent[at, row] for at in range(N_PAIRS)]
         result = []
         for a in range(6):
             total = entries[PAIR_OF[a, 0]] * strain[0]
             for b in range(1, 6):
                 total = total + entries[PAIR_OF[a, b]] * strain[b]
-            result.append(total)
+            result.append(jnp.where(present, total, 0.0))
         return result
 
     def first_image(row, carry):
         low, before = carry
         high = pairs_of(v0, row + 1)
         present = valid_elements & (row + index_y > 0)
-        strain = [jnp.where(present, value, 0.0) for value in strain_row(low, high)]
-        parts = force_parts(stress_row(row, strain))
+        parts = force_parts(stress_row(row, strain_row(low, high), present))
         keep = keep_of(row)
         for m in range(3):
             force = force_of(parts[m][0] + before[m][0], parts[m][1] + before[m][1])
@@ -478,8 +488,7 @@
     def second_image(row, carry):
         low, before, sums = carry
         high = pairs_of(v1, row + 1)
-        strain = [jnp.where(own_elements, value, 0.0) for value in strain_row(low, high)]
-        parts = force_parts(stress_row(row, strain))
+        parts = force_parts(stress_row(row, strain_row(low, high), own_elements))
         rr, r_ar, ar_ar, ar_aar = sums
         for m in range(3):
             here, image = v0[m, row], v1[m, row]
@@ -551,7 +560,10 @@
         all_rows(image_row)
         rest = gathered.at[parity, 0 : peers - 1]
         pltpu.make_async_copy(rest, rest, all_recv.at[parity]).wait()
-        totals = jnp.sum(gathered[parity], axis=0)
+        totals = [jnp.sum(gathered[parity, at : at + 16], axis=0) for at in range(0, peers, 16)]
+        while len(totals) > 1:
+            totals = [a + b for a, b in zip(totals[0::2], totals[1::2])]
+        totals = totals[0]
         rr2, m1, m2, m3 = [
             jnp.sum(jnp.where(lane == at, totals, 0.0), axis=1, keepdims=True) for at in range(4)
         ]
@@ -594,20 +606,36 @@
     none = jnp.zeros((1, 1), F32)
     lax.fori_loop(0, OUTER, outer, (none, none, none, none + 1.0))
 
-    stores = []
-    for i in range(NODES_X):
-        for m in range(3):
-            stores.append(pltpu.make_async_copy(x.at[m, 1:18, i + 1 : i + 2], increment_hbm.at[i, :, m : m + 1], out_sem.at[0, m, i]))
-            stores.append(pltpu.make_async_copy(v0.at[m, 1:18, i + 1 : i + 2], residual_hbm.at[i, :, m : m + 1], out_sem.at[1, m, i]))
+    stores = [
+        pltpu.make_async_copy(x, increment_hbm, out_sem.at[0]),
+        pltpu.make_async_copy(v0, residual_hbm, out_sem.at[1]),
+    ]
     for copy in stores:
         copy.start()
     for copy in stores:
         copy.wait()
 
 
+def place_kernel(increment_in, residual_in, increment_out, residual_out, sem):
+    copies = []
+    for at, (source, target) in enumerate(((increment_in, increment_out), (residual_in, residual_out))):
+        for i in range(NODES_X):
+            for m in range(3):
+                copies.append(
+                    pltpu.make_async_copy(
+                        source.at[m, 1:18, i + 1 : i + 2], target.at[i, :, m : m + 1], sem.at[at, m, i]
+                    )
+                )
+    for copy in copies:
+        copy.start()
+    for copy in copies:
+        copy.wait()
+
+
 def solution(mesh):
     size_x, size_y = mesh.shape["gx"], mesh.shape["gy"]
     peers = size_x * size_y
+    held = jax.ShapeDtypeStruct((3, ROWS, SUB, NZ), F32)
     field = jax.ShapeDtypeStruct((NODES_X, NODES_Y, 3, NZ), F32)
 
     def vmem(*shape, dtype=F32):
@@ -618,27 +646,25 @@
 
     dma = pltpu.SemaphoreType.DMA
     scratch = [
+        vmem(1, SLOTS, dtype=jnp.int32), vmem(1, 1, dtype=jnp.int32), vmem(6, HID), vmem(42, HID),
         node(3), node(3), node(), node(), node(3), vmem(BY, SUB, NZ), vmem(HIDDEN_LAYERS, HID, HID),
         vmem(6, BY, SUB, NZ), vmem(NZ, SLOTS, dtype=BF16), vmem(SLOTS, NZ, dtype=BF16),
         vmem(COLUMNS, SLOTS, dtype=BF16), vmem(BY * SUB, SLOTS), vmem(SLOTS, 128, dtype=BF16),
         vmem(128, SLOTS), vmem(32, SLOTS), vmem(2 * GROUP * COLUMNS, SLOTS, dtype=BF16),
-        vmem(N_SCATTER, BY, SUB, NZ),
+        vmem(GROUP, BY, SUB, NZ),
         vmem(N_PAIRS, BY + 2, SUB, NZ),
         node(3), node(3), node(3), node(3), node(3), node(3), node(3),
         node(2, 3, 3), node(2, 3), vmem(2, peers, 1, 128),
-        dma((9, 5)), dma((2, 3, 5)), dma((8,)), dma((8,)), dma((3, 8)), dma((3, 8)),
+        dma((10, 5)), dma((2,)), dma((8,)), dma((8,)), dma((3, 8)), dma((3, 8)),
         dma((2, 8)), dma((2, 8)), dma((2, 8)), dma((2, 8)), dma((2,)), dma((2,)),
     ]
 
     def body(u_now, load, mass, modulus, plastic_ids, plastic_count, w_in, w_hidden, w_head):
         hbm = pl.BlockSpec(memory_space=pl.ANY)
-        local = pl.BlockSpec(memory_space=pltpu.VMEM)
         increment, residual = pl.pallas_call(
             lambda *refs: kernel(size_x, size_y, *refs),
-            out_shape=(field, field),
-            in_specs=[
-                hbm, hbm, hbm, hbm, local, pl.BlockSpec(memory_space=pltpu.SMEM), local, hbm, local,
-            ],
+            out_shape=(held, held),
+            in_specs=[hbm] * 9,
             out_specs=(hbm, hbm),
             scratch_shapes=scratch,
             compiler_params=pltpu.CompilerParams(
@@ -648,6 +674,13 @@
             u_now.transpose(1, 2, 0, 3), load.transpose(1, 2, 0, 3), mass, modulus,
             plastic_ids.reshape(1, SLOTS), plastic_count, w_in, w_hidden, w_head.T,
         )
+        increment, residual = pl.pallas_call(
+            place_kernel,
+            out_shape=(field, field),
+            in_specs=[pl.BlockSpec(memory_space=pltpu.VMEM)] * 2,
+            out_specs=(hbm, hbm),
+            scratch_shapes=[dma((2, 3, 5))],
+        )(increment, residual)
         return increment.transpose(2, 0, 1, 3), residual.transpose(2, 0, 1, 3)
 
     split_field = P(None, "gx", "gy", None)

time: 61.6 us -> 58.4 us (0.948)
  local copies, waits for them, and re-layouts: 3.54 us -> 0 us
    unnamed x2 -> x0, local copies, waits for them, and re-layouts: 3.54 us -> none
    pallas_call x1 -> x2, Pallas kernels: 56.5 us -> 57 us  [the longest x1 54.8 us: body(): pl.pallas_call(lambda *refs: kernel(size_x, size_y, *refs), out_shape=(he...]
where the time goes in v3:
time: 58.4 us; the launch traced here: 58.3 us
  Pallas kernels  57 us (98%)
  between operations  1.29 us (2%)
    pallas_call x1, Pallas kernels, body(): pl.pallas_call(lambda *refs: kernel(size_x, size_y, *refs), out_shape=(he...  54.8 us
    pallas_call x1, Pallas kernels, body(): pl.pallas_call(place_kernel, out_shape=(field, field), in_specs=[pl.Block...  2.19 us

profile of v3, /device:TPU:1, one launch (start us, length us, event | category | flops | bytes accessed | tf_op | source)
XLA Modules:
  0.0 58.3 jit_solution(17765112116774542835)
XLA Ops:
  1.3 54.8 %shard_map.104 = (f32[3,19,8,256]{3,2,1,0:T(8,128)}, f32[3,19,8,256]{3,2,1,0:T(8,128)}) custom-call(f32[5,17,3,256]{3,2,1,0:T(4,128)} %bitcast.6, f32[5,17,3,256]{3,2,1,0:T(4,128)} %bitcast.7, f32[5,17,256]{2,1,0:T(8,128)} %refs_2_.1, f32[4,16,256]{2,1,0:T(8,128)} %refs_3_.1, s32[1,1024]{1,0:T(1,128)} %bitcast.9, s32[1,1]{1,0:T(1,128)S(6)} %copy.11.refs_5_, ...), custom_call_target="tpu_custom_call" | custom-call | tf_op jit(solution)/shard_map/pallas_call | solution.py:664
  56.1 2.2 %shard_map.105 = (f32[5,17,3,256]{3,2,1,0:T(4,128)}, f32[5,17,3,256]{3,2,1,0:T(4,128)}) custom-call(f32[3,19,8,256]{3,2,1,0:T(8,128)} %get-tuple-element.6.increment_in, f32[3,19,8,256]{3,2,1,0:T(8,128)} %get-tuple-element.7.residual_in), custom_call_target="tpu_custom_call" | custom-call | tf_op jit(solution)/shard_map/pallas_call | solution.py:677

commit v4 on v3

--- a/solution.py
+++ b/solution.py
@@ -28,7 +28,8 @@
 N_SCATTER = 28
 LIVE, FIRST_PAIR = 6, 7
 
-DIRECTIONS = [(dx, dy) for dx in (-1, 0, 1) for dy in (-1, 0, 1) if (dx, dy) != (0, 0)]
+DIRECTIONS = [(dx, dy) for dx in (-1, 1) for dy in (-1, 1)] + [(0, -1), (0, 1), (-1, 0), (1, 0)]
+FACES = 2
 
 
 def iso(a, b):
@@ -150,7 +151,7 @@
     u_hbm, load_hbm, mass_hbm, modulus_hbm, ids_hbm, count_hbm, w_in_hbm, w_hidden_hbm, w_head_hbm,
     increment_hbm, residual_hbm,
     ids_ref, count_ref, w_in_ref, w_head_ref, ux, lx, mass_part, mass_full, mass_rx, modulus, weights,
-    strain_now, onehot_k, onehot_kt, onehot_r, onehot_r8, inputs_t, out_t, values, lhs, scattered,
+    strain_now, packed, onehot_k, onehot_kt, onehot_r, inputs_t, out_t, values, lhs, scattered,
     tangent,
     v0, v1, v2, q1, q0, d1, x, sum_rx, copy_rx, gathered,
     load_sem, out_sem, mass_send, mass_recv, tan_send, tan_recv,
@@ -217,9 +218,6 @@
     onehot_r[...] = jnp.where(
         lax.broadcasted_iota(jnp.int32, (COLUMNS, SLOTS), 0) == at_j * BX + at_i, live, 0.0
     ).astype(BF16)
-    onehot_r8[...] = jnp.where(
-        lax.broadcasted_iota(jnp.int32, (BY * SUB, SLOTS), 0) == at_j * SUB + at_i + 1, 1.0, 0.0
-    )
     k_column = jnp.broadcast_to(at_k.astype(F32), (128, SLOTS)).T
     lane_k = lax.broadcasted_iota(jnp.int32, (SLOTS, 128), 1).astype(F32)
     onehot_kt[:, 0:128] = jnp.where(k_column == lane_k, 1.0, 0.0).astype(BF16)
@@ -243,9 +241,19 @@
 
     picked = []
     for n in range(6):
-        high, low = split(strain_now[n].reshape(BY * SUB, NZ))
-        rows = mm(high, onehot_k[...]) + mm(low, onehot_k[...])
-        picked.append(jnp.sum(rows * onehot_r8[...], axis=0, keepdims=True))
+        for g in range(BY // 2):
+            pair = jnp.where(
+                sub < BX,
+                pltpu.roll(strain_now[n, 2 * g], SUB - 1, 0),
+                pltpu.roll(strain_now[n, 2 * g + 1], BX - 1, 0),
+            )
+            high = pair.astype(BF16).astype(F32)
+            packed[n * COLUMNS + g * SUB : n * COLUMNS + (g + 1) * SUB] = high
+            packed[(6 + n) * COLUMNS + g * SUB : (6 + n) * COLUMNS + (g + 1) * SUB] = pair - high
+    at_slots = mm(packed[...].astype(BF16), onehot_k[...])
+    for n in range(6):
+        rows = at_slots[n * COLUMNS : (n + 1) * COLUMNS] + at_slots[(6 + n) * COLUMNS : (7 + n) * COLUMNS]
+        picked.append(jnp.sum(rows * onehot_r[...].astype(F32), axis=0, keepdims=True))
     eps = jnp.concatenate(picked + [jnp.zeros((2, SLOTS), F32)], axis=0)
     eps_high = eps.astype(BF16).astype(F32)
     stacked = jnp.concatenate(
@@ -521,7 +529,7 @@
             v2[m, NODES_Y] = force
             ar_aar = ar_aar + jnp.where(own_planes, image * force, 0.0)
         summed = sum_copies(sum_parity)
-        for copy in summed:
+        for copy in summed[:-FACES]:
             copy.start()
 
         message = jnp.zeros((1, 128), F32)
@@ -539,6 +547,8 @@
                 all_send.at[parity], all_recv.at[parity],
                 device_id=device, device_id_type=MESH,
             ).start()
+        for copy in summed[-FACES:]:
+            copy.start()
         for copy in exact + summed:
             copy.wait()
 
@@ -607,8 +617,12 @@
     lax.fori_loop(0, OUTER, outer, (none, none, none, none + 1.0))
 
     stores = [
-        pltpu.make_async_copy(x, increment_hbm, out_sem.at[0]),
-        pltpu.make_async_copy(v0, residual_hbm, out_sem.at[1]),
+        pltpu.make_async_copy(
+            source.at[m, 1:18, i + 1 : i + 2], target.at[i, :, m : m + 1], out_sem.at[at, m, i]
+        )
+        for at, (source, target) in enumerate(((x, increment_hbm), (v0, residual_hbm)))
+        for i in range(NODES_X)
+        for m in range(3)
     ]
     for copy in stores:
         copy.start()
@@ -617,15 +631,10 @@
 
 
 def place_kernel(increment_in, residual_in, increment_out, residual_out, sem):
-    copies = []
-    for at, (source, target) in enumerate(((increment_in, increment_out), (residual_in, residual_out))):
-        for i in range(NODES_X):
-            for m in range(3):
-                copies.append(
-                    pltpu.make_async_copy(
-                        source.at[m, 1:18, i + 1 : i + 2], target.at[i, :, m : m + 1], sem.at[at, m, i]
-                    )
-                )
+    copies = [
+        pltpu.make_async_copy(increment_in, increment_out, sem.at[0]),
+        pltpu.make_async_copy(residual_in, residual_out, sem.at[1]),
+    ]
     for copy in copies:
         copy.start()
     for copy in copies:
@@ -635,7 +644,6 @@
 def solution(mesh):
     size_x, size_y = mesh.shape["gx"], mesh.shape["gy"]
     peers = size_x * size_y
-    held = jax.ShapeDtypeStruct((3, ROWS, SUB, NZ), F32)
     field = jax.ShapeDtypeStruct((NODES_X, NODES_Y, 3, NZ), F32)
 
     def vmem(*shape, dtype=F32):
@@ -648,14 +656,14 @@
     scratch = [
         vmem(1, SLOTS, dtype=jnp.int32), vmem(1, 1, dtype=jnp.int32), vmem(6, HID), vmem(42, HID),
         node(3), node(3), node(), node(), node(3), vmem(BY, SUB, NZ), vmem(HIDDEN_LAYERS, HID, HID),
-        vmem(6, BY, SUB, NZ), vmem(NZ, SLOTS, dtype=BF16), vmem(SLOTS, NZ, dtype=BF16),
-        vmem(COLUMNS, SLOTS, dtype=BF16), vmem(BY * SUB, SLOTS), vmem(SLOTS, 128, dtype=BF16),
+        vmem(6, BY, SUB, NZ), vmem(12 * COLUMNS, NZ), vmem(NZ, SLOTS, dtype=BF16), vmem(SLOTS, NZ, dtype=BF16),
+        vmem(COLUMNS, SLOTS, dtype=BF16), vmem(SLOTS, 128, dtype=BF16),
         vmem(128, SLOTS), vmem(32, SLOTS), vmem(2 * GROUP * COLUMNS, SLOTS, dtype=BF16),
         vmem(GROUP, BY, SUB, NZ),
         vmem(N_PAIRS, BY + 2, SUB, NZ),
         node(3), node(3), node(3), node(3), node(3), node(3), node(3),
         node(2, 3, 3), node(2, 3), vmem(2, peers, 1, 128),
-        dma((10, 5)), dma((2,)), dma((8,)), dma((8,)), dma((3, 8)), dma((3, 8)),
+        dma((10, 5)), dma((2, 3, 5)), dma((8,)), dma((8,)), dma((3, 8)), dma((3, 8)),
         dma((2, 8)), dma((2, 8)), dma((2, 8)), dma((2, 8)), dma((2,)), dma((2,)),
     ]
 
@@ -663,7 +671,7 @@
         hbm = pl.BlockSpec(memory_space=pl.ANY)
         increment, residual = pl.pallas_call(
             lambda *refs: kernel(size_x, size_y, *refs),
-            out_shape=(held, held),
+            out_shape=(field, field),
             in_specs=[hbm] * 9,
             out_specs=(hbm, hbm),
             scratch_shapes=scratch,
@@ -679,7 +687,7 @@
             out_shape=(field, field),
             in_specs=[pl.BlockSpec(memory_space=pltpu.VMEM)] * 2,
             out_specs=(hbm, hbm),
-            scratch_shapes=[dma((2, 3, 5))],
+            scratch_shapes=[dma((2,))],
         )(increment, residual)
         return increment.transpose(2, 0, 1, 3), residual.transpose(2, 0, 1, 3)
 

time: 58.4 us -> 58.2 us (level)
  no operation moved by 1% of the time
where the time goes in v4:
time: 58.2 us; the launch traced here: 58 us
  Pallas kernels  56.7 us (97%)
  between operations  1.29 us (2%)
    pallas_call x1, Pallas kernels, body(): pl.pallas_call(lambda *refs: kernel(size_x, size_y, *refs), out_shape=(fi...  54.8 us
    pallas_call x1, Pallas kernels, body(): pl.pallas_call(place_kernel, out_shape=(field, field), in_specs=[pl.Block...  1.95 us

profile of v4, /device:TPU:1, one launch (start us, length us, event | category | flops | bytes accessed | tf_op | source)
XLA Modules:
  0.0 58.0 jit_solution(17241313049574644355)
XLA Ops:
  1.3 54.8 %shard_map.104 = (f32[5,17,3,256]{3,2,1,0:T(4,128)}, f32[5,17,3,256]{3,2,1,0:T(4,128)}) custom-call(f32[5,17,3,256]{3,2,1,0:T(4,128)} %bitcast.6, f32[5,17,3,256]{3,2,1,0:T(4,128)} %bitcast.7, f32[5,17,256]{2,1,0:T(8,128)} %refs_2_.1, f32[4,16,256]{2,1,0:T(8,128)} %refs_3_.1, s32[1,1024]{1,0:T(1,128)} %bitcast.9, s32[1,1]{1,0:T(1,128)S(6)} %copy.11.refs_5_, ...), custom_call_target="tpu_custom_call" | custom-call | tf_op jit(solution)/shard_map/pallas_call | solution.py:672
  56.1 1.9 %shard_map.105 = (f32[5,17,3,256]{3,2,1,0:T(4,128)}, f32[5,17,3,256]{3,2,1,0:T(4,128)}) custom-call(f32[5,17,3,256]{3,2,1,0:T(4,128)} %get-tuple-element.6.increment_in, f32[5,17,3,256]{3,2,1,0:T(4,128)} %get-tuple-element.7.residual_in), custom_call_target="tpu_custom_call" | custom-call | tf_op jit(solution)/shard_map/pallas_call | solution.py:685

commit v5 on v4

--- a/solution.py
+++ b/solution.py
@@ -6,7 +6,8 @@
 from jax.sharding import PartitionSpec as P
 
 MESH = pl.DeviceIdType.MESH
-F32, BF16 = jnp.float32, jnp.bfloat16
+F32, BF16, F8 = jnp.float32, jnp.bfloat16, jnp.float8_e4m3fn
+HIGH_SCALE, LOW_SCALE = 16.0, 16.0 * 512.0
 LAME_FIRST = 0.3 / (1.3 * 0.4)
 LAME_SECOND = 1.0 / 2.6
 
@@ -39,13 +40,15 @@
 
 
 def z_next(values):
-    lane = lax.broadcasted_iota(jnp.int32, values.shape, 1)
-    return jnp.where(lane == NZ - 1, 0.0, pltpu.roll(values, NZ - 1, 1))
+    edge = lax.broadcasted_iota(jnp.int32, (values.shape[0], 128), 1) == 127
+    low, high = [pltpu.roll(values[:, at : at + 128], 127, 1) for at in (0, 128)]
+    return jnp.concatenate([jnp.where(edge, high, low), jnp.where(edge, 0.0, high)], axis=1)
 
 
 def z_prev(values):
-    lane = lax.broadcasted_iota(jnp.int32, values.shape, 1)
-    return jnp.where(lane == 0, 0.0, pltpu.roll(values, 1, 1))
+    edge = lax.broadcasted_iota(jnp.int32, (values.shape[0], 128), 1) == 0
+    low, high = [pltpu.roll(values[:, at : at + 128], 1, 1) for at in (0, 128)]
+    return jnp.concatenate([jnp.where(edge, 0.0, low), jnp.where(edge, low, high)], axis=1)
 
 
 def x_pairs(values):
@@ -272,20 +275,29 @@
         (from_out == (to_row // 8) * 6 + to_row % 8) & (to_row % 8 < 6) & (to_row < 56), 1.0, 0.0
     ).astype(BF16)
     head_high, head_low = split(w_head_ref[...])
-    head_high = mm(place, head_high).T.astype(BF16)
-    head_low = mm(place, head_low).T.astype(BF16)
+    head = (mm(place, head_high) + mm(place, head_low)).T
+    def product(hidden, parts):
+        high, mixed_weight = parts
+        hidden_high = hidden.astype(BF16)
+        low = hidden - hidden_high.astype(F32)
+        mixed = jnp.concatenate([(low * LOW_SCALE).astype(F8), (hidden * HIGH_SCALE).astype(F8)], axis=1)
+        return mm(hidden_high, high) + mm(mixed, mixed_weight) * (1.0 / (HIGH_SCALE * LOW_SCALE))
+
+    def narrow(weight):
+        high = weight.astype(BF16)
+        low = weight - high.astype(F32)
+        return high, jnp.concatenate(
+            [(weight * HIGH_SCALE).astype(F8), (low * LOW_SCALE).astype(F8)], axis=0
+        )
+
     halves = []
     for layer in range(HIDDEN_LAYERS):
         weight_loads[layer].wait()
-        halves.append(split(weights[layer]))
-
-    def product(hidden, parts):
-        high, low = split(hidden)
-        return mm(high, parts[0]) + (mm(low, parts[0]) + mm(high, parts[1]))
+        halves.append(narrow(weights[layer]))
 
     half = SLOTS // 2
     left, right = mm(inputs_t[0:half], w_first), mm(inputs_t[half:SLOTS], w_first)
-    for parts in halves + [(head_high, head_low)]:
+    for parts in halves + [narrow(head)]:
         left = product(jnp.tanh(left), parts)
         right = product(jnp.tanh(right), parts)
     out_t[:, 0:half] = left.T
@@ -313,16 +325,18 @@
             factor[a] * factor[b], axis=0, keepdims=True
         ) * (1.0 / 6.0)
 
-    def scatter_group(at):
+    def spread_ready(at):
         for n in range(GROUP):
             high, low = split(values[at * GROUP + n : at * GROUP + n + 1])
             rows = onehot_r[...]
-            lhs[n * COLUMNS : (n + 1) * COLUMNS] = rows * high
-            lhs[(GROUP + n) * COLUMNS : (GROUP + n + 1) * COLUMNS] = rows * low
-        if at == 0:
-            spread = mm(lhs[...], onehot_kt[...])
-            return spread[: GROUP * COLUMNS] + spread[GROUP * COLUMNS :]
-        return mm(lhs[: GROUP * COLUMNS], onehot_kt[...]) + mm(lhs[GROUP * COLUMNS :], onehot_kt[...])
+            lhs[at, n * COLUMNS : (n + 1) * COLUMNS] = rows * high
+            lhs[at, (GROUP + n) * COLUMNS : (GROUP + n + 1) * COLUMNS] = rows * low
+
+    def spread_group(at):
+        if at < N_SCATTER // GROUP - 1:
+            spread_ready(at + 1)
+        spread = mm(lhs[at], onehot_kt[...])
+        return spread[: GROUP * COLUMNS] + spread[GROUP * COLUMNS :]
 
     def element_rows(spread, n, g):
         start = n * COLUMNS + g * SUB
@@ -410,7 +424,8 @@
             v2[m, row] = jnp.where(own_planes, lx[m, row] - force, 0.0)
         return [(parts[m][0], parts[m][2]) for m in range(3)]
 
-    spread = scatter_group(0)
+    spread_ready(0)
+    spread = spread_group(0)
     for n in range(GROUP):
         for g in range(BY // 2):
             for odd, entry in enumerate(element_rows(spread, n, g)):
@@ -428,7 +443,7 @@
     tangent_copies = []
     planes = slice(1, 1 + BX)
     for group in range(N_PAIRS // GROUP):
-        spread = scatter_group(group + 1)
+        spread = spread_group(group + 1)
         for g in range(BY // 2):
             scales = [modulus[2 * g + odd] * (1.0 / 16.0) for odd in range(2)]
             bases = [scales[odd] * (1.0 - 0.75 * scattered[LIVE, 2 * g + odd]) for odd in range(2)]
@@ -658,7 +673,7 @@
         node(3), node(3), node(), node(), node(3), vmem(BY, SUB, NZ), vmem(HIDDEN_LAYERS, HID, HID),
         vmem(6, BY, SUB, NZ), vmem(12 * COLUMNS, NZ), vmem(NZ, SLOTS, dtype=BF16), vmem(SLOTS, NZ, dtype=BF16),
         vmem(COLUMNS, SLOTS, dtype=BF16), vmem(SLOTS, 128, dtype=BF16),
-        vmem(128, SLOTS), vmem(32, SLOTS), vmem(2 * GROUP * COLUMNS, SLOTS, dtype=BF16),
+        vmem(128, SLOTS), vmem(32, SLOTS), vmem(N_SCATTER // GROUP, 2 * GROUP * COLUMNS, SLOTS, dtype=BF16),
         vmem(GROUP, BY, SUB, NZ),
         vmem(N_PAIRS, BY + 2, SUB, NZ),
         node(3), node(3), node(3), node(3), node(3), node(3), node(3),

time: 58.2 us -> 57.1 us (0.981)
  Pallas kernels: 56.7 us -> 55.7 us
    pallas_call x1, Pallas kernels: 54.8 us -> 53.7 us  [body(): pl.pallas_call(lambda *refs: kernel(size_x, size_y, *refs), out_shape=(fi...]
where the time goes in v5:
time: 57.1 us; the launch traced here: 57 us
  Pallas kernels  55.7 us (98%)
  between operations  1.29 us (2%)
    pallas_call x1, Pallas kernels, body(): pl.pallas_call(lambda *refs: kernel(size_x, size_y, *refs), out_shape=(fi...  53.7 us
    pallas_call x1, Pallas kernels, body(): pl.pallas_call(place_kernel, out_shape=(field, field), in_specs=[pl.Block...  1.95 us

profile of v5, /device:TPU:1, one launch (start us, length us, event | category | flops | bytes accessed | tf_op | source)
XLA Modules:
  0.0 57.0 jit_solution(4531238060937045750)
XLA Ops:
  1.3 53.7 %shard_map.104 = (f32[5,17,3,256]{3,2,1,0:T(4,128)}, f32[5,17,3,256]{3,2,1,0:T(4,128)}) custom-call(f32[5,17,3,256]{3,2,1,0:T(4,128)} %bitcast.6, f32[5,17,3,256]{3,2,1,0:T(4,128)} %bitcast.7, f32[5,17,256]{2,1,0:T(8,128)} %refs_2_.1, f32[4,16,256]{2,1,0:T(8,128)} %refs_3_.1, s32[1,1024]{1,0:T(1,128)} %bitcast.9, s32[1,1]{1,0:T(1,128)S(6)} %copy.11.refs_5_, ...), custom_call_target="tpu_custom_call" | custom-call | tf_op jit(solution)/shard_map/pallas_call | solution.py:687
  55.0 1.9 %shard_map.105 = (f32[5,17,3,256]{3,2,1,0:T(4,128)}, f32[5,17,3,256]{3,2,1,0:T(4,128)}) custom-call(f32[5,17,3,256]{3,2,1,0:T(4,128)} %get-tuple-element.6.increment_in, f32[5,17,3,256]{3,2,1,0:T(4,128)} %get-tuple-element.7.residual_in), custom_call_target="tpu_custom_call" | custom-call | tf_op jit(solution)/shard_map/pallas_call | solution.py:700

commit v6 on v5

--- a/solution.py
+++ b/solution.py
@@ -280,8 +280,8 @@
         high, mixed_weight = parts
         hidden_high = hidden.astype(BF16)
         low = hidden - hidden_high.astype(F32)
-        mixed = jnp.concatenate([(low * LOW_SCALE).astype(F8), (hidden * HIGH_SCALE).astype(F8)], axis=1)
-        return mm(hidden_high, high) + mm(mixed, mixed_weight) * (1.0 / (HIGH_SCALE * LOW_SCALE))
+        mixed = jnp.concatenate([(low * (LOW_SCALE / HIGH_SCALE)).astype(F8), hidden.astype(F8)], axis=1)
+        return mm(hidden_high, high) + mm(mixed, mixed_weight) * (1.0 / LOW_SCALE)
 
     def narrow(weight):
         high = weight.astype(BF16)
@@ -403,7 +403,7 @@
             body(row)
             return carry
 
-        by_rows(2, NODES_Y, 5, inner, 0)
+        by_rows(2, NODES_Y, 3, inner, 0)
 
     def stress_now(row):
         scale = 0.25 * modulus[row]
@@ -623,7 +623,7 @@
                 d1[m, row] = d3
             return unused
 
-        by_rows(0, ROWS - 1, 6, update_row, 0)
+        by_rows(0, ROWS - 1, 3, update_row, 0)
         update_row(ROWS - 1, 0)
         pltpu.make_async_copy(rest, rest, all_send.at[parity]).wait()
         return be2, 1.0 / a3, 1.0 / a2, rr3

time: 57.1 us -> 57.1 us (level)
  no operation moved by 1% of the time
where the time goes in v6:
time: 57.1 us; the launch traced here: 56.9 us
  Pallas kernels  55.6 us (97%)
  between operations  1.29 us (2%)
    pallas_call x1, Pallas kernels, body(): pl.pallas_call(lambda *refs: kernel(size_x, size_y, *refs), out_shape=(fi...  53.7 us
    pallas_call x1, Pallas kernels, body(): pl.pallas_call(place_kernel, out_shape=(field, field), in_specs=[pl.Block...  1.95 us

profile of v6, /device:TPU:1, one launch (start us, length us, event | category | flops | bytes accessed | tf_op | source)
XLA Modules:
  0.0 56.9 jit_solution(12872955283089031634)
XLA Ops:
  1.3 53.7 %shard_map.104 = (f32[5,17,3,256]{3,2,1,0:T(4,128)}, f32[5,17,3,256]{3,2,1,0:T(4,128)}) custom-call(f32[5,17,3,256]{3,2,1,0:T(4,128)} %bitcast.6, f32[5,17,3,256]{3,2,1,0:T(4,128)} %bitcast.7, f32[5,17,256]{2,1,0:T(8,128)} %refs_2_.1, f32[4,16,256]{2,1,0:T(8,128)} %refs_3_.1, s32[1,1024]{1,0:T(1,128)} %bitcast.9, s32[1,1]{1,0:T(1,128)S(6)} %copy.11.refs_5_, ...), custom_call_target="tpu_custom_call" | custom-call | tf_op jit(solution)/shard_map/pallas_call | solution.py:687
  55.0 1.9 %shard_map.105 = (f32[5,17,3,256]{3,2,1,0:T(4,128)}, f32[5,17,3,256]{3,2,1,0:T(4,128)}) custom-call(f32[5,17,3,256]{3,2,1,0:T(4,128)} %get-tuple-element.6.increment_in, f32[5,17,3,256]{3,2,1,0:T(4,128)} %get-tuple-element.7.residual_in), custom_call_target="tpu_custom_call" | custom-call | tf_op jit(solution)/shard_map/pallas_call | solution.py:700

commit v7 on v6

--- a/solution.py
+++ b/solution.py
@@ -645,15 +645,21 @@
         copy.wait()
 
 
-def place_kernel(increment_in, residual_in, increment_out, residual_out, sem):
-    copies = [
-        pltpu.make_async_copy(increment_in, increment_out, sem.at[0]),
-        pltpu.make_async_copy(residual_in, residual_out, sem.at[1]),
+def place_kernel(increment_in, residual_in, increment_out, residual_out, held, load_sem, store_sem):
+    pieces = [
+        (source.at[i], held.at[at, i], target.at[i], load_sem.at[at, i], store_sem.at[at, i])
+        for at, (source, target) in enumerate(((increment_in, increment_out), (residual_in, residual_out)))
+        for i in range(NODES_X)
     ]
-    for copy in copies:
-        copy.start()
-    for copy in copies:
-        copy.wait()
+    loads = [pltpu.make_async_copy(source, slot, arrived) for source, slot, _, arrived, _ in pieces]
+    stores = [pltpu.make_async_copy(slot, target, left) for _, slot, target, _, left in pieces]
+    for load in loads:
+        load.start()
+    for load, store in zip(loads, stores):
+        load.wait()
+        store.start()
+    for store in stores:
+        store.wait()
 
 
 def solution(mesh):
@@ -700,9 +706,9 @@
         increment, residual = pl.pallas_call(
             place_kernel,
             out_shape=(field, field),
-            in_specs=[pl.BlockSpec(memory_space=pltpu.VMEM)] * 2,
+            in_specs=[hbm, hbm],
             out_specs=(hbm, hbm),
-            scratch_shapes=[dma((2,))],
+            scratch_shapes=[vmem(2, NODES_X, NODES_Y, 3, NZ), dma((2, NODES_X)), dma((2, NODES_X))],
         )(increment, residual)
         return increment.transpose(2, 0, 1, 3), residual.transpose(2, 0, 1, 3)
 

time: 57.1 us -> 57.1 us (level)
  no operation moved by 1% of the time
where the time goes in v7:
time: 57.1 us; the launch traced here: 57 us
  Pallas kernels  55.7 us (98%)
  between operations  1.29 us (2%)
    pallas_call x1, Pallas kernels, body(): pl.pallas_call(lambda *refs: kernel(size_x, size_y, *refs), out_shape=(fi...  53.7 us
    pallas_call x1, Pallas kernels, body(): pl.pallas_call(place_kernel, out_shape=(field, field), in_specs=[hbm, hbm...  1.99 us

profile of v7, /device:TPU:1, one launch (start us, length us, event | category | flops | bytes accessed | tf_op | source)
XLA Modules:
  0.0 57.0 jit_solution(16740157518927141072)
XLA Ops:
  1.3 53.7 %shard_map.104 = (f32[5,17,3,256]{3,2,1,0:T(4,128)}, f32[5,17,3,256]{3,2,1,0:T(4,128)}) custom-call(f32[5,17,3,256]{3,2,1,0:T(4,128)} %bitcast.6, f32[5,17,3,256]{3,2,1,0:T(4,128)} %bitcast.7, f32[5,17,256]{2,1,0:T(8,128)} %refs_2_.1, f32[4,16,256]{2,1,0:T(8,128)} %refs_3_.1, s32[1,1024]{1,0:T(1,128)} %bitcast.9, s32[1,1]{1,0:T(1,128)S(6)} %copy.11.refs_5_, ...), custom_call_target="tpu_custom_call" | custom-call | tf_op jit(solution)/shard_map/pallas_call | solution.py:693
  55.0 2.0 %shard_map.105 = (f32[5,17,3,256]{3,2,1,0:T(4,128)}, f32[5,17,3,256]{3,2,1,0:T(4,128)}) custom-call(f32[5,17,3,256]{3,2,1,0:T(4,128)} %get-tuple-element.6.increment_in, f32[5,17,3,256]{3,2,1,0:T(4,128)} %get-tuple-element.7.residual_in), custom_call_target="tpu_custom_call" | custom-call | tf_op jit(solution)/shard_map/pallas_call | solution.py:706
